TPU v7x, 32 devices: a whole 2x2x4 slice. The times are simulated.
32 devices in a mesh: dp: 8 (over y, x, core), mp: 4 (over z).
Axes of the slice: x: 2, y: 2, z: 4, core: 2. Of those that a mesh axis runs over, the one named last changes fastest.
Arguments:
- hidden: bfloat16 [256, 16, 2048], P('dp', None, 'mp'), may hold values from -6 to 6
- norm_gain: bfloat16 [2048], P('mp'), may hold values from 0.099609375 to 1.8984375
- in_x: bfloat16 [2048, 4096], P('dp', 'mp'), may hold values from -0.125 to 0.125
- in_z: bfloat16 [2048, 4096], P('dp', 'mp'), may hold values from -0.125 to 0.125
- conv_weight: float32 [4, 4096], P(None, 'mp'), may hold values from -3 to 3
- conv_bias: float32 [4096], P('mp'), may hold values from -3 to 3
- x_proj: bfloat16 [4096, 160], P(('mp', 'dp')), may hold values from -0.09375 to 0.09375
- dt_proj: bfloat16 [128, 4096], P('dp', 'mp'), may hold values from -0.5 to 0.5
- dt_bias: float32 [4096], P('mp'), may hold values from -5 to -1
- a_log: float32 [16, 4096], P(None, 'mp'), may hold values from 0 to 2.77
- skip: float32 [4096], P('mp'), may hold values from 0.5 to 1.5
- out_proj: bfloat16 [4096, 2048], P('mp', 'dp'), may hold values from -0.09375 to 0.09375
- state_pool: float32 [320, 16, 4096], P('dp', None, 'mp'), may hold values from -6 to 6
- conv_pool: float32 [320, 3, 4096], P('dp', None, 'mp'), may hold values from -6 to 6
- permutation: int32 [256], P('dp'), may hold values from 0 to 255, as said below
- page_table: int32 [256], P('dp'), may hold values from 0 to 319, as said below
- accepted: int32 [256], P('dp'), may hold values from 1 to 16
Outputs:
- verified: bfloat16 [256, 16, 2048], P('dp', None, 'mp')
- new_state_pool: float32 [320, 16, 4096], P('dp', None, 'mp')
- new_conv_pool: float32 [320, 3, 4096], P('dp', None, 'mp')
Inputs may be any that keep to these rules, and one draw needn't show every extreme that they name: `permutation`: A request at position j of the block of dp index d goes to position j of the block of dp index (d + o) mod 8, where the shift o depends only on j mod 8 and takes 8 different values; so each dp index sends exactly 4 requests to each of 8 dp indices and receives 32. `page_table`: the requests of dp index d use distinct slots among the 40 slots d * 40 .. (d + 1) * 40 - 1.
All inputs are finite; a program needn't handle non-finite values.
Results may differ from a plain program's by a relative error of at most 0.0065.
Values may be sent and summed in bfloat16 or wider, within the bound.
A program may use at most 128 MiB of HBM per device.

v0:
```python
import jax
import jax.numpy as jnp
from jax import lax
from jax.sharding import PartitionSpec as P

EPS = 1e-05


def route_plan(permutation, count, peers):
    capacity = count // min(count, peers)
    target = permutation // count
    order = jnp.arange(count)
    earlier = (target[:, None] == target[None, :]) & (order[None, :] < order[:, None])
    rank_within = jnp.sum(earlier.astype(jnp.int32), axis=1)
    position = target * capacity + rank_within
    match = position[None, :] == jnp.arange(peers * capacity)[:, None]
    filled = jnp.any(match, axis=1)
    source = jnp.argmax(match, axis=1)
    return (position, filled, source)


def pack_rows(values, filled, source):
    picked = jnp.take(values, source, axis=0)
    shape = (filled.shape[0],) + (1,) * (values.ndim - 1)
    return jnp.where(filled.reshape(shape), picked, jnp.zeros_like(picked))


def unpack_rows(values, arrived, count):
    match = arrived[None, :] == jnp.arange(count)[:, None]
    index = jnp.argmax(match, axis=1)
    return jnp.take(values, index, axis=0)


def write_pool(pool, slot_local, values):
    match = slot_local[None, :] == jnp.arange(pool.shape[0])[:, None]
    filled = jnp.any(match, axis=1)
    index = jnp.argmax(match, axis=1)
    return jnp.where(filled[:, None, None], jnp.take(values, index, axis=0), pool)


def verify_layer(
    hidden,
    norm_gain,
    in_x,
    in_z,
    conv_weight,
    conv_bias,
    x_proj,
    dt_proj,
    dt_bias,
    a_log,
    skip,
    out_proj,
    caches,
    accepted,
):
    count, drafts, width_local = hidden.shape
    tokens = count * drafts
    inner_local = in_x.shape[1]
    state_count = a_log.shape[0]
    taps = conv_weight.shape[0]
    rank = x_proj.shape[1] - 2 * state_count
    full, gain_full = (
        lax.all_gather(hidden, "mp", axis=2, tiled=True),
        lax.all_gather(norm_gain, "mp", axis=0, tiled=True),
    )
    rows = full.reshape(tokens, -1).astype(jnp.float32)
    scale = lax.rsqrt(jnp.mean(rows * rows, axis=1, keepdims=True) + EPS)
    normed = (rows * scale * gain_full.astype(jnp.float32)).astype(jnp.bfloat16)
    columns = normed
    x_wide = jnp.dot(
        columns, lax.all_gather(in_x, "dp", axis=0, tiled=True), preferred_element_type=jnp.float32
    )
    z_wide = jnp.dot(
        columns, lax.all_gather(in_z, "dp", axis=0, tiled=True), preferred_element_type=jnp.float32
    )
    x_part = x_wide.astype(jnp.bfloat16)
    z_part = z_wide.astype(jnp.bfloat16)
    states = caches[:, :state_count, :]
    edges = caches[:, state_count:, :]
    padded = jnp.concatenate(
        [edges, x_part.astype(jnp.float32).reshape(count, drafts, inner_local)], axis=1
    )
    mixed = conv_bias + jnp.zeros((count, drafts, inner_local), jnp.float32)
    for offset in range(taps):
        mixed = mixed + conv_weight[offset] * padded[:, offset : offset + drafts, :]
    inputs = jax.nn.silu(mixed).astype(jnp.bfloat16)
    flat_inputs = inputs.reshape(tokens, inner_local)
    piece = lax.all_gather(x_proj, "dp", axis=0, tiled=True)
    columns = flat_inputs
    low_sum = jnp.dot(columns, piece[:, :rank], preferred_element_type=jnp.float32)
    both_sum = jnp.einsum("ks,tk->st", piece[:, rank:], columns, preferred_element_type=jnp.float32)
    low_full, both = lax.psum((low_sum, both_sum), "mp")
    low_half = low_full.astype(jnp.bfloat16)
    columns = low_half
    delta = jnp.dot(
        columns,
        lax.all_gather(dt_proj, "dp", axis=0, tiled=True),
        preferred_element_type=jnp.float32,
    )
    delta = jax.nn.softplus(delta + dt_bias).reshape(count, drafts, inner_local)
    decay_rate = -jnp.exp(a_log)
    inputs_wide = inputs.astype(jnp.float32)
    driven = delta * inputs_wide
    b_time = both[:state_count].reshape(state_count, count, drafts).transpose(2, 1, 0)
    c_time = both[state_count:].reshape(state_count, count, drafts).transpose(2, 1, 0)

    def advance(carry, slices):
        state, kept = carry
        step_delta, step_drive, step_b, step_c, index = slices
        state = (
            jnp.exp(step_delta[:, None, :] * decay_rate[None]) * state
            + step_drive[:, None, :] * step_b[:, :, None]
        )
        output = jnp.sum(state * step_c[:, :, None], axis=1)
        kept = jnp.where((accepted - 1 == index)[:, None, None], state, kept)
        return ((state, kept), output)

    (final_state, kept), outputs = lax.scan(
        advance,
        (states, states),
        (
            delta.transpose(1, 0, 2),
            driven.transpose(1, 0, 2),
            b_time,
            c_time,
            jnp.arange(drafts, dtype=jnp.int32),
        ),
    )
    outputs = outputs.transpose(1, 0, 2)
    gate_wide = z_part.astype(jnp.float32).reshape(count, drafts, inner_local)
    gated = (
        ((outputs + skip * inputs_wide) * jax.nn.silu(gate_wide))
        .astype(jnp.bfloat16)
        .reshape(tokens, inner_local)
    )
    index = accepted[:, None] + jnp.arange(taps - 1, dtype=jnp.int32)[None, :]
    new_edges = jnp.take_along_axis(padded, index[:, :, None], axis=1)
    new_caches = jnp.concatenate([kept, new_edges], axis=1)
    terms = jnp.dot(
        gated,
        lax.all_gather(out_proj, "dp", axis=1, tiled=True),
        preferred_element_type=jnp.float32,
    )
    summed = lax.psum_scatter(terms, "mp", scatter_dimension=1, tiled=True)
    result = (summed + hidden.reshape(tokens, width_local).astype(jnp.float32)).astype(jnp.bfloat16)
    return (result.reshape(count, drafts, width_local), new_caches)


def on_device(
    hidden,
    norm_gain,
    in_x,
    in_z,
    conv_weight,
    conv_bias,
    x_proj,
    dt_proj,
    dt_bias,
    a_log,
    skip,
    out_proj,
    state_pool,
    conv_pool,
    permutation,
    page_table,
    accepted,
):
    count = hidden.shape[0]
    state_count = state_pool.shape[1]
    pool_count = state_pool.shape[0]
    peers = lax.axis_size("dp")
    slot_local = page_table % pool_count
    caches = jnp.concatenate(
        [jnp.take(state_pool, slot_local, axis=0), jnp.take(conv_pool, slot_local, axis=0)], axis=1
    )
    position, filled, source = route_plan(permutation, count, peers)
    arrival_slot = permutation % count
    details = jnp.stack([arrival_slot, accepted], axis=1).astype(jnp.float32)
    details_sent = jnp.where(filled[:, None], jnp.take(details, source, axis=0), -1.0)
    got_hidden = lax.all_to_all(
        pack_rows(hidden, filled, source), "dp", split_axis=0, concat_axis=0, tiled=True
    )
    got_caches, got_details = (
        lax.all_to_all(
            pack_rows(caches, filled, source), "dp", split_axis=0, concat_axis=0, tiled=True
        ),
        lax.all_to_all(details_sent, "dp", split_axis=0, concat_axis=0, tiled=True),
    )
    arrived = got_details[:, 0].astype(jnp.int32)
    local_hidden = unpack_rows(got_hidden, arrived, count)
    local_caches = unpack_rows(got_caches, arrived, count)
    local_accept = unpack_rows(got_details[:, 1], arrived, count).astype(jnp.int32)
    verified, new_caches = verify_layer(
        local_hidden,
        norm_gain,
        in_x,
        in_z,
        conv_weight,
        conv_bias,
        x_proj,
        dt_proj,
        dt_bias,
        a_log,
        skip,
        out_proj,
        local_caches,
        local_accept,
    )
    returned = jnp.take(new_caches, jnp.maximum(arrived, 0), axis=0)
    returned = jnp.where((arrived >= 0)[:, None, None], returned, jnp.zeros_like(returned))
    back = lax.all_to_all(
        returned.astype(jnp.bfloat16), "dp", split_axis=0, concat_axis=0, tiled=True
    ).astype(returned.dtype)
    settled = jnp.take(back, position, axis=0)
    new_state_pool = write_pool(state_pool, slot_local, settled[:, :state_count])
    new_conv_pool = write_pool(conv_pool, slot_local, settled[:, state_count:])
    return (verified, new_state_pool, new_conv_pool)


def solution(mesh):
    return jax.shard_map(
        on_device,
        mesh=mesh,
        in_specs=(
            P("dp", None, "mp"),
            P("mp"),
            P("dp", "mp"),
            P("dp", "mp"),
            P(None, "mp"),
            P("mp"),
            P(("mp", "dp"), None),
            P("dp", "mp"),
            P("mp"),
            P(None, "mp"),
            P("mp"),
            P("mp", "dp"),
            P("dp", None, "mp"),
            P("dp", None, "mp"),
            P("dp"),
            P("dp"),
            P("dp"),
        ),
        out_specs=(P("dp", None, "mp"), P("dp", None, "mp"), P("dp", None, "mp")),
        check_vma=False,
    )
```

profile of v0, /device:TPU:9, one launch (start us, length us, event | category | flops | bytes accessed | tf_op | source)
XLA Modules:
  0.0 382.7 jit_solution(14049422077861747644)
XLA Ops:
  11.7 4.4 %all-to-all-start.1 = ((f32[8,4,2]{1,2,0:T(2,128)}), f32[8,4,2]{1,2,0:T(2,128)S(1)}, u32[]{:S(2)}, u32[]{:S(2)}) async-start(f32[8,4,2]{1,2,0:T(2,128)} %copy.94), calls=%async_computation.1 | async-start | bytes 16384 | tf_op jit(solution)/shard_map/all_to_all | solution.py:188
  17.6 2.5 all-to-all-done.1
  20.1 4.7 %all-to-all-start.2 = ((bf16[32,16,512]{2,1,0:T(8,128)(2,1)}), bf16[32,16,512]{2,1,0:T(8,128)(2,1)}, u32[]{:S(2)}, u32[]{:S(2)}) async-start(bf16[32,16,512]{2,1,0:T(8,128)(2,1)} %select_select_fusion.3), calls=%async_computation.2 | async-start | bytes 1048576 | tf_op jit(solution)/shard_map/all_to_all | solution.py:181
  26.9 4.8 %all-to-all-done.2 = bf16[32,16,512]{2,1,0:T(8,128)(2,1)} async-done(((bf16[32,16,512]{2,1,0:T(8,128)(2,1)}), bf16[32,16,512]{2,1,0:T(8,128)(2,1)}, u32[]{:S(2)}, u32[]{:S(2)}) %all-to-all-start.2) | async-done | bytes 524320 | tf_op jit(solution)/shard_map/all_to_all | solution.py:181
  31.7 2.4 gather_fusion.10
  34.1 2.0 broadcast_select_fusion.4
  37.7 2.0 gather_fusion
  41.5 2.0 pad_maximum_fusion
  43.6 2.7 gather_fusion.7
  46.3 2.4 select_select_fusion.1
  48.7 6.8 %all-to-all-start = ((f32[32,19,1024]{2,1,0:T(8,128)}), f32[32,19,1024]{2,1,0:T(8,128)S(1)}, u32[]{:S(2)}, u32[]{:S(2)}) async-start(f32[32,19,1024]{2,1,0:T(8,128)} %select_select_fusion.1), calls=%async_computation | async-start | bytes 6291456 | tf_op jit(solution)/shard_map/all_to_all | solution.py:185
  55.5 10.2 %all-gather = bf16[4,1,512]{2,1,0:T(2,128)(2,1)S(1)} all-gather(bf16[1,1,512]{2,1,0:T(2,128)(2,1)S(1)} %reshape.339), channel_id=1, replica_groups=mesh['dp'=8,'mp'=4] {'mp'}, dimensions={0}, use_global_device_ids=true | all-gather | bytes 5120 | tf_op jit(solution)/shard_map/all_gather | solution.py:65
  65.7 32.1 %all_gather.24 = bf16[1024,160]{0,1:T(8,128)(2,1)S(1)} all-gather(bf16[128,160]{0,1:T(8,128)(2,1)S(1)} %copy-done.12), channel_id=1, replica_groups=mesh['dp'=8,'mp'=4] {'dp'}, dimensions={0}, use_global_device_ids=true | all-gather | bytes 368640 | tf_op jit(solution)/shard_map/all_gather | solution.py:89
  97.9 2.6 gather_fusion.8
  100.5 2.3 broadcast_select_fusion.2
  102.8 1.7 copy-done.5
  104.9 2.1 multiply_reduce_fusion.1
  107.0 3.9 %fusion.1 = bf16[512,2048]{1,0:T(8,128)(2,1)} fusion(f32[2048]{0:T(1024)S(1)} %bitcast.89, f32[512]{0:T(512)S(1)} %rsqrt.12, bf16[32,16,2048]{2,1,0:T(8,128)(2,1)} %all-gather.6.cloned.1.call-done), kind=kLoop, calls=%fused_computation.25 | loop fusion | flops 4194304 | bytes 4204544 | tf_op jit(solution)/shard_map/convert_element_type | solution.py:69
  110.9 11.4 %all-gather.8.cloned.1.call-done = bf16[2048,1024]{1,0:T(8,128)(2,1)} async-done(((bf16[256,1024]{1,0:T(8,128)(2,1)}), bf16[2048,1024]{1,0:T(8,128)(2,1)}) %all-gather.8.cloned.1.call-update) | async-done | bytes 4194320 | tf_op jit(solution)/shard_map/all_gather | solution.py:72
  122.3 5.2 %convolution_convert_fusion.1 = bf16[512,1024]{1,0:T(8,128)(2,1)S(1)} fusion(bf16[512,2048]{1,0:T(8,128)(2,1)} %fusion.1, bf16[2048,1024]{1,0:T(8,128)(2,1)} %all-gather.8.cloned.1.call-done), kind=kOutput, calls=%fused_computation.52 | convolution fusion | flops 2148007936 | bytes 7340032 | tf_op jit(solution)/shard_map/dot_general | solution.py:71
  128.9 2.6 multiply_convert_fusion
  131.5 1.9 copy.100
  136.1 10.3 %all_gather.25 = bf16[128,1024]{1,0:T(8,128)(2,1)} all-gather(bf16[16,1024]{1,0:T(8,128)(2,1)S(1)} %copy-done.13), channel_id=1, replica_groups=mesh['dp'=8,'mp'=4] {'dp'}, dimensions={0}, use_global_device_ids=true | all-gather | bytes 294912 | tf_op jit(solution)/shard_map/all_gather | solution.py:98
  146.5 2.0 fusion.26
  149.7 18.4 %all-reduce.4 = bf16[512,128]{1,0:T(8,128)(2,1)S(1)} all-reduce(f32[512,128]{1,0:T(8,128)} %fusion.12), channel_id=1, replica_groups=mesh['dp'=8,'mp'=4] {'mp'}, use_global_device_ids=true, to_apply=%region_5.8 | all-reduce | flops 65536 | bytes 393216 | tf_op jit(solution)/shard_map/psum | solution.py:93
  168.1 2.3 compare_select_fusion
  170.3 4.6 %fusion.3 = (f32[16,32,1024]{2,1,0:T(8,128)}, f32[16,32,1024]{2,1,0:T(8,128)}) fusion(bf16[32,16,1024]{2,0,1:T(8,128)(2,1)} %multiply_convert_fusion, f32[32,16,1024]{2,1,0:T(8,128)S(1)} %bitcast.81), kind=kLoop, calls=%fused_computation.35 | loop fusion | flops 1048576 | bytes 7340032 | tf_op jit(solution)/shard_map/transpose | solution.py:124
  175.0 5.2 %convolution_convert_fusion = bf16[512,1024]{1,0:T(8,128)(2,1)S(1)} fusion(bf16[512,2048]{1,0:T(8,128)(2,1)} %fusion.1, bf16[2048,1024]{1,0:T(8,128)(2,1)} %all-gather.10.cloned.1.call-done), kind=kOutput, calls=%fused_computation.51 | convolution fusion | flops 2148007936 | bytes 7340032 | tf_op jit(solution)/shard_map/dot_general | solution.py:74
  180.2 1.6 convert.5
  181.7 13.4 %all-reduce.3.cloned.1.call-done = f32[32,512]{1,0:T(8,128)} async-done(((f32[32,512]{1,0:T(8,128)}), f32[32,512]{1,0:T(8,128)}) %all-reduce.3.cloned.1.call-update) | async-done | bytes 65552 | tf_op jit(solution)/shard_map/psum | solution.py:93
  198.1 85.4 %while.16 = (s32[]{:T(128)}, f32[32,16,1024]{2,1,0:T(8,128)S(1)}, bf16[32,16,1024]{2,1,0:T(8,128)(2,1)S(1)}, f32[16,32,1024]{2,1,0:T(8,128)}, f32[16,32,1024]{2,...) while((s32[]{:T(128)}, f32[32,16,1024]{2,1,0:T(8,128)S(1)}, ...), condition=%wide.region_9.12_spmd, body=%wide.region_7.11_spmd.sunk | while | flops 3637314 | bytes 9646925 | solution.py:119
  199.9 1.2 multiply_reduce_fusion.3
  283.5 4.1 %fusion.6 = bf16[32,16,1024]{2,0,1:T(8,128)(2,1)S(1)} fusion(bf16[32,16,1024]{2,0,1:T(8,128)(2,1)} %multiply_convert_fusion, f32[16,32,1024]{2,1,0:T(8,128)} %get-tuple-element.148, f32[32,16,1024]{2,1,0:T(8,128)} %convert.5, f32[1024]{0:T(1024)S(1)} %copy-done.21), kind=kLoop, calls=%fused_computation.38 | loop fusion | flops 4718592 | bytes 6295552 | tf_op jit(solution)/shard_map/convert_element_type | solution.py:134
  288.3 6.5 %fusion.29 = f32[512,2048]{1,0:T(8,128)} fusion(bf16[512,1024]{1,0:T(8,128)(2,1)S(1)} %bitcast.84, bf16[1024,2048]{1,0:T(8,128)(2,1)} %all-gather.12.cloned.1.call-done), kind=kOutput, calls=%fused_computation.123 | convolution fusion | flops 2147483648 | bytes 9437184 | tf_op jit(solution)/shard_map/dot_general | solution.py:140
  296.2 3.3 gather_fusion.6
  300.0 1.4 pad_maximum_fusion.1
  301.4 2.1 gather_fusion.11
  303.5 2.0 fusion.2
  305.4 6.6 %all-to-all-start.3 = ((bf16[32,19,1024]{2,1,0:T(8,128)(2,1)}), bf16[32,19,1024]{2,1,0:T(8,128)(2,1)S(1)}, u32[]{:S(2)}, u32[]{:S(2)}) async-start(bf16[32,19,1024]{2,1,0:T(8,128)(2,1)} %fusion.2), calls=%async_computation.4 | async-start | bytes 3145728 | tf_op jit(solution)/shard_map/all_to_all | solution.py:212
  312.2 17.5 %all-to-all-done.3 = bf16[32,19,1024]{2,1,0:T(8,128)(2,1)S(1)} async-done(((bf16[32,19,1024]{2,1,0:T(8,128)(2,1)}), bf16[32,19,1024]{2,1,0:T(8,128)(2,1)S(1)}, u32[]{:S(2)}, u32[]{:S(2)}) %all-to-all-start.3) | async-done | bytes 1245216 | tf_op jit(solution)/shard_map/all_to_all | solution.py:212
  329.6 2.0 convert_element_type.95
  331.7 2.6 gather_fusion.12
  336.0 2.2 gather_fusion.4
  338.2 3.0 gather_fusion.5
  341.2 1.5 copy_select_fusion
  343.8 3.7 select_select_fusion.2
  347.4 26.1 %reduce-scatter.2.cloned.1.call-done = f32[512,512]{1,0:T(8,128)} async-done(((f32[512,2048]{1,0:T(8,128)}), f32[512,512]{1,0:T(8,128)}) %reduce-scatter.2.cloned.1.call-update) | async-done | bytes 1048592 | tf_op jit(solution)/shard_map/reduce_scatter | solution.py:145
  373.6 2.3 fusion.11
  (260 shorter events, 108.9 us)
Async XLA Ops:
  7.2 8.9 %copy-start = (bf16[32,16,512]{2,1,0:T(8,128)(2,1)S(1)}, bf16[32,16,512]{2,1,0:T(8,128)(2,1)}, u32[]{:S(2)}) copy-start(bf16[32,16,512]{2,1,0:T(8,128)(2,1)} %param.23) | copy-start | bytes 1572868
  8.6 0.8 copy-start.25
  11.7 8.4 %all-to-all-start.1 = ((f32[8,4,2]{1,2,0:T(2,128)}), f32[8,4,2]{1,2,0:T(2,128)S(1)}, u32[]{:S(2)}, u32[]{:S(2)}) async-start(f32[8,4,2]{1,2,0:T(2,128)} %copy.94), calls=%async_computation.1 | async-start | bytes 16384 | tf_op jit(solution)/shard_map/all_to_all | solution.py:188
  20.1 11.6 %all-to-all-start.2 = ((bf16[32,16,512]{2,1,0:T(8,128)(2,1)}), bf16[32,16,512]{2,1,0:T(8,128)(2,1)}, u32[]{:S(2)}, u32[]{:S(2)}) async-start(bf16[32,16,512]{2,1,0:T(8,128)(2,1)} %select_select_fusion.3), calls=%async_computation.2 | async-start | bytes 1048576 | tf_op jit(solution)/shard_map/all_to_all | solution.py:181
  24.8 80.0 %all-gather.6.cloned.1.call-start = ((), (), s32[]{:S(2)}) async-start(), calls=%async_computation.5 | async-start | bytes 2621440 | tf_op jit(solution)/shard_map/all_gather | solution.py:64
  24.9 12.7 %copy-start.19 = (f32[32,2]{0,1:T(2,128)}, f32[32,2]{0,1:T(2,128)S(1)}, u32[]{:S(2)}) copy-start(f32[32,2]{0,1:T(2,128)S(1)} %all_to_all.17) | copy-start | bytes 772
  25.6 12.0 %copy-start.15 = (s32[1024]{0:T(1024)}, s32[1024]{0:T(1024)S(1)}, u32[]{:S(2)}) copy-start(s32[1024]{0:T(1024)S(1)} %pad_clamp_fusion.3) | copy-start | bytes 12292
  25.6 12.0 %copy-start.28 = (s32[32]{0:T(128)S(1)}, s32[32]{0:T(128)}, u32[]{:S(2)}) copy-start(s32[32]{0:T(128)} %param.38) | copy-start | bytes 388
  25.6 12.1 %copy-start.9 = (f32[40,16,1024]{2,1,0:T(8,128)S(1)}, f32[40,16,1024]{2,1,0:T(8,128)}, u32[]{:S(2)}) copy-start(f32[40,16,1024]{2,1,0:T(8,128)} %param.35) | copy-start | bytes 7864324
  26.9 12.8 %copy-start.16 = (pred[32]{0:T(512)(128)(4,1)}, pred[32]{0:T(512)(128)(4,1)S(1)}, u32[]{:S(2)}) copy-start(pred[32]{0:T(512)(128)(4,1)S(1)} %get-tuple-element.245) | copy-start | bytes 100
  36.1 86.2 %all-gather.8.cloned.1.call-start = ((), (), s32[]{:S(2)}) async-start(), calls=%async_computation.6 | async-start | bytes 4718592 | tf_op jit(solution)/shard_map/all_gather | solution.py:72
  36.9 138.1 %all-gather.10.cloned.1.call-start = ((), (), s32[]{:S(2)}) async-start(), calls=%async_computation.8 | async-start | bytes 4718592 | tf_op jit(solution)/shard_map/all_gather | solution.py:75
  37.6 2.1 copy-start.29
  37.7 2.0 copy-start.2
  39.7 1.6 copy-start.10
  48.7 6.8 %copy-start.24 = (bf16[512]{0:T(512)(128)(2,1)S(1)}, bf16[512]{0:T(512)(128)(2,1)}, u32[]{:S(2)}) copy-start(bf16[512]{0:T(512)(128)(2,1)} %param.24) | copy-start | bytes 3076
  48.7 17.1 %copy-start.12 = (bf16[128,160]{0,1:T(8,128)(2,1)S(1)}, bf16[128,160]{0,1:T(8,128)(2,1)}, u32[]{:S(2)}) copy-start(bf16[128,160]{0,1:T(8,128)(2,1)} %param.29) | copy-start | bytes 122884
  48.7 49.2 %copy-start.14 = (f32[4,1024]{1,0:T(4,128)S(1)}, f32[4,1024]{1,0:T(4,128)}, u32[]{:S(2)}) copy-start(f32[4,1024]{1,0:T(4,128)} %param.27) | copy-start | bytes 49156
  48.7 49.2 %all-to-all-start = ((f32[32,19,1024]{2,1,0:T(8,128)}), f32[32,19,1024]{2,1,0:T(8,128)S(1)}, u32[]{:S(2)}, u32[]{:S(2)}) async-start(f32[32,19,1024]{2,1,0:T(8,128)} %select_select_fusion.1), calls=%async_computation | async-start | bytes 6291456 | tf_op jit(solution)/shard_map/all_to_all | solution.py:185
  55.5 139.7 %all-reduce.3.cloned.1.call-start = ((), (), s32[]{:S(2)}) async-start(), calls=%async_computation.7 | async-start | bytes 131072 | tf_op jit(solution)/shard_map/psum | solution.py:93
  97.9 2.6 copy-start.17
  102.8 1.7 copy-start.5
  127.7 1.3 copy-start.18
  128.9 6.5 %copy-start.4 = (f32[32,19,1024]{2,0,1:T(8,128)}, f32[32,19,1024]{2,0,1:T(8,128)S(1)}, u32[]{:S(2)}) copy-start(f32[32,19,1024]{2,0,1:T(8,128)S(1)} %copy_dynamic-update-slice_fusion) | copy-start | bytes 7471108
  131.5 4.6 %copy-start.13 = (bf16[16,1024]{1,0:T(8,128)(2,1)S(1)}, bf16[16,1024]{1,0:T(8,128)(2,1)}, u32[]{:S(2)}) copy-start(bf16[16,1024]{1,0:T(8,128)(2,1)} %param.30) | copy-start | bytes 98308
  131.5 15.0 %copy-start.11 = (f32[16,1024]{1,0:T(8,128)S(1)}, f32[16,1024]{1,0:T(8,128)}, u32[]{:S(2)}) copy-start(f32[16,1024]{1,0:T(8,128)} %param.32) | copy-start | bytes 196612
  133.4 1.0 copy-start.7
  135.5 152.8 %all-gather.12.cloned.1.call-start = ((), (), s32[]{:S(2)}) async-start(), calls=%async_computation.9 | async-start | bytes 4718592 | tf_op jit(solution)/shard_map/all_gather | solution.py:142
  136.1 237.5 %reduce-scatter.2.cloned.1.call-start = ((), (), s32[]{:S(2)}) async-start(), calls=%async_computation.10 | async-start | bytes 5242880 | tf_op jit(solution)/shard_map/reduce_scatter | solution.py:145
  146.5 2.0 copy-start.8
  146.5 21.6 %copy-start.27 = (f32[1024]{0:T(1024)S(1)}, f32[1024]{0:T(1024)}, u32[]{:S(2)}) copy-start(f32[1024]{0:T(1024)} %param.31) | copy-start | bytes 12292
  180.1 18.0 %copy-start.23 = (s32[32]{0:T(128)S(1)}, s32[32]{0:T(128)}, u32[]{:S(2)}) copy-start(s32[32]{0:T(128)} %get-tuple-element.357) | copy-start | bytes 388
  198.1 85.4 %copy-start.21 = (f32[1024]{0:T(1024)S(1)}, f32[1024]{0:T(1024)}, u32[]{:S(2)}) copy-start(f32[1024]{0:T(1024)} %param.33) | copy-start | bytes 12292
  294.8 0.6 copy-start.30
  294.8 1.4 copy-start.20
  305.4 6.6 %copy-start.26 = (s32[32]{0:T(128)S(1)}, s32[32]{0:T(128)}, u32[]{:S(2)}) copy-start(s32[32]{0:T(128)} %copy-done.25) | copy-start | bytes 388
  305.4 24.2 %all-to-all-start.3 = ((bf16[32,19,1024]{2,1,0:T(8,128)(2,1)}), bf16[32,19,1024]{2,1,0:T(8,128)(2,1)S(1)}, u32[]{:S(2)}, u32[]{:S(2)}) async-start(bf16[32,19,1024]{2,1,0:T(8,128)(2,1)} %fusion.2), calls=%async_computation.4 | async-start | bytes 3145728 | tf_op jit(solution)/shard_map/all_to_all | solution.py:212
  331.7 2.7 copy-start.22
  336.0 5.2 %copy-start.3 = (f32[40,3,1024]{2,0,1:T(8,128)S(1)}, f32[40,3,1024]{2,0,1:T(8,128)}, u32[]{:S(2)}) copy-start(f32[40,3,1024]{2,0,1:T(8,128)} %param.36) | copy-start | bytes 1474564
  338.2 5.6 %copy-start.6 = (f32[40,16,1024]{2,1,0:T(8,128)S(1)}, f32[40,16,1024]{2,1,0:T(8,128)}, u32[]{:S(2)}) copy-start(f32[40,16,1024]{2,1,0:T(8,128)} %gather_fusion.4) | copy-start | bytes 7864324
  343.8 32.1 %copy-start.1 = (bf16[32,16,512]{2,1,0:T(8,128)(2,1)S(1)}, bf16[32,16,512]{2,1,0:T(8,128)(2,1)}, u32[]{:S(2)}) copy-start(bf16[32,16,512]{2,1,0:T(8,128)(2,1)} %param.23) | copy-start | bytes 1572868
Sparse Core Ops, SparseCore 0:
  36.2 45.8 all-gather.5
  84.0 38.1 all-gather.7
  124.2 36.7 all-gather.9
  163.6 31.4 all-reduce.2
  197.0 39.6 all-gather.11
  294.9 78.5 reduce-scatter.1
where the time goes:
time: 388 us; the launch traced here: 383 us
  local copies, waits for them, and re-layouts  89.1 us (23%)
  other arithmetic  85.6 us (22%)
  waiting for transfers between devices  77.6 us (20%)
  blocking collectives  71.1 us (18%)
  starting transfers between devices  22.7 us (6%)
  matrix products  21.3 us (5%)
  between operations  14.7 us (4%)
    all_gather x1, blocking collectives, verify_layer(): piece = lax.all_gather(x_proj, 'dp', axis=0, tiled=True)  32.1 us
    reduce_scatter x1, waiting for transfers between devices, verify_layer(): summed = lax.psum_scatter(terms, 'mp', scatter_dimension=1, tiled=True)  26.1 us
    reduce_sum x16, other arithmetic, advance(): output = jnp.sum(state * step_c[:, :, None], axis=1)  19.9 us
    psum x1, blocking collectives, verify_layer(): low_full, both = lax.psum((low_sum, both_sum), 'mp')  18.4 us
    all_to_all x1, waiting for transfers between devices, on_device(): lax.all_to_all(returned.astype(jnp.bfloat16), 'dp', split_axis=0, concat_...  17.5 us
    mul x16, local copies, waits for them, and re-layouts, advance(): step_drive[:, None, :] * step_b[:, :, None]  15.9 us
    psum x1, waiting for transfers between devices, verify_layer(): low_full, both = lax.psum((low_sum, both_sum), 'mp')  13.4 us
    mul x16, local copies, waits for them, and re-layouts, advance(): output = jnp.sum(state * step_c[:, :, None], axis=1)  11.9 us
  transfers between devices with their start and end apart: 10, of which 6 were waited for; matrix products, arithmetic and copies ran while one was open for 46% of the time, Pallas kernels for 0%

commit v1 on v0

v1 whole, which is shorter than its diff:
```python
import functools

import jax
import jax.numpy as jnp
from jax import lax
from jax.experimental import pallas as pl
from jax.experimental.pallas import tpu as pltpu
from jax.sharding import PartitionSpec as P

EPS = 1e-05
LANES = 128
VMEM_BYTES = 48 * 1024 * 1024


def whole(count, smem=0):
    vmem = pl.BlockSpec(memory_space=pltpu.VMEM)
    return [pl.BlockSpec(memory_space=pltpu.SMEM)] * smem + [vmem] * (count - smem)


def conv_kernel(
    slot_ref, accepted_ref, x_ref, pool_ref, weight_ref, bias_ref, proj_ref,
    inputs_ref, partial_ref, new_pool_ref, padded,
):
    count, drafts, _ = x_ref.shape
    taps = weight_ref.shape[0]
    new_pool_ref[...] = pool_ref[...]

    def one(r, _):
        slot = slot_ref[r]
        padded[0 : taps - 1, :] = pool_ref[slot]
        padded[taps - 1 : taps - 1 + drafts, :] = x_ref[r].astype(jnp.float32)
        mixed = bias_ref[...] + weight_ref[0:1, :] * padded[0:drafts, :]
        for k in range(1, taps):
            mixed = mixed + weight_ref[k : k + 1, :] * padded[k : k + drafts, :]
        inputs_ref[r] = (mixed / (1.0 + jnp.exp(-mixed))).astype(jnp.bfloat16)
        for k in range(taps - 1):
            new_pool_ref[slot, k : k + 1, :] = padded[pl.ds(accepted_ref[r] + k, 1), :]
        return 0

    lax.fori_loop(0, count, one, 0)
    inputs = inputs_ref[...].reshape(count * drafts, -1)
    partial_ref[...] = jnp.dot(inputs, proj_ref[...], preferred_element_type=jnp.float32)


def conv_branch(x_part, conv_pool, conv_weight, conv_bias, x_proj, slot, accepted):
    count, drafts, inner = x_part.shape
    return pl.pallas_call(
        conv_kernel,
        out_shape=(
            jax.ShapeDtypeStruct(x_part.shape, jnp.bfloat16),
            jax.ShapeDtypeStruct((count * drafts, x_proj.shape[1]), jnp.float32),
            jax.ShapeDtypeStruct(conv_pool.shape, jnp.float32),
        ),
        in_specs=whole(7, smem=2),
        out_specs=tuple(whole(3)),
        scratch_shapes=[pltpu.VMEM((24, inner), jnp.float32)],
        compiler_params=pltpu.CompilerParams(vmem_limit_bytes=VMEM_BYTES),
        cost_estimate=pl.CostEstimate(flops=200_000_000, bytes_accessed=4_000_000, transcendentals=600_000),
    )(slot, accepted, x_part, conv_pool, conv_weight, conv_bias.reshape(1, -1), x_proj)


def scan_kernel(
    slot_ref, accepted_ref, low_ref, proj_ref, dt_bias_ref, a_log_ref, skip_ref,
    inputs_ref, z_ref, both_ref, pool_ref,
    gated_ref, new_pool_ref, decay, delta, drive, rows,
):
    count, drafts, inner = inputs_ref.shape
    states = a_log_ref.shape[0]
    blocks = inner // LANES
    new_pool_ref[...] = pool_ref[...]
    decay[...] = -jnp.exp(a_log_ref[...])

    def one(r, _):
        slot = slot_ref[r]
        last = accepted_ref[r] - 1
        raw = jnp.dot(low_ref[r], proj_ref[...], preferred_element_type=jnp.float32) + dt_bias_ref[...]
        step = jnp.maximum(raw, 0.0) + jnp.log1p(jnp.exp(-jnp.abs(raw)))
        delta[...] = step
        drive[...] = step * inputs_ref[r].astype(jnp.float32)
        both = both_ref[r]
        state = [pool_ref[slot, :, j * LANES : (j + 1) * LANES] for j in range(blocks)]
        kept = list(state)
        for t in range(drafts):
            column = jnp.broadcast_to(both[:, t : t + 1], (2 * states, LANES))
            b_wide, c_wide = column[:states], column[states:]
            chosen = last == t
            for j in range(blocks):
                lanes = slice(j * LANES, (j + 1) * LANES)
                grown = jnp.exp(delta[t : t + 1, lanes] * decay[:, lanes]) * state[j]
                state[j] = grown + drive[t : t + 1, lanes] * b_wide
                rows[t : t + 1, lanes] = jnp.sum(state[j] * c_wide, axis=0, keepdims=True)
                kept[j] = jnp.where(chosen, state[j], kept[j])
        for j in range(blocks):
            new_pool_ref[slot, :, j * LANES : (j + 1) * LANES] = kept[j]
        z = z_ref[r].astype(jnp.float32)
        mixed = rows[...] + skip_ref[...] * inputs_ref[r].astype(jnp.float32)
        gated_ref[r] = (mixed * (z / (1.0 + jnp.exp(-z)))).astype(jnp.bfloat16)
        return 0

    lax.fori_loop(0, count, one, 0)


def scan_branch(low, dt_proj, dt_bias, a_log, skip, inputs, z_part, both, state_pool, slot, accepted):
    count, drafts, inner = inputs.shape
    states = a_log.shape[0]
    return pl.pallas_call(
        scan_kernel,
        out_shape=(
            jax.ShapeDtypeStruct(inputs.shape, jnp.bfloat16),
            jax.ShapeDtypeStruct(state_pool.shape, jnp.float32),
        ),
        in_specs=whole(11, smem=2),
        out_specs=tuple(whole(2)),
        scratch_shapes=[
            pltpu.VMEM((states, inner), jnp.float32),
            pltpu.VMEM((drafts, inner), jnp.float32),
            pltpu.VMEM((drafts, inner), jnp.float32),
            pltpu.VMEM((drafts, inner), jnp.float32),
        ],
        compiler_params=pltpu.CompilerParams(vmem_limit_bytes=VMEM_BYTES),
        cost_estimate=pl.CostEstimate(flops=100_000_000, bytes_accessed=10_000_000, transcendentals=9_000_000),
    )(
        slot, accepted, low, dt_proj, dt_bias.reshape(1, -1), a_log, skip.reshape(1, -1),
        inputs, z_part, both, state_pool,
    )


def route(rows, permutation, count, peers):
    period = min(count, peers)
    capacity = count // period
    me = lax.axis_index("dp")
    shift = (permutation[:period] // count - me + peers) % peers
    chunks = jnp.arange(peers)
    hit = chunks[:, None] == (me + shift[None, :]) % peers
    klass = jnp.argmax(hit, axis=1)
    grouped = rows.reshape((capacity, period) + rows.shape[1:]).swapaxes(0, 1)
    sent = jnp.take(grouped, klass, axis=0)
    got = lax.all_to_all(sent, "dp", split_axis=0, concat_axis=0, tiled=True)
    source = (me - shift + peers) % peers
    placed = jnp.take(got, source, axis=0)
    return placed.swapaxes(0, 1).reshape(rows.shape)


def on_device(
    hidden, norm_gain, in_x, in_z, conv_weight, conv_bias, x_proj, dt_proj, dt_bias,
    a_log, skip, out_proj, state_pool, conv_pool, permutation, page_table, accepted,
):
    count, drafts, width_local = hidden.shape
    tokens = count * drafts
    inner_local = in_x.shape[1]
    states = a_log.shape[0]
    rank = x_proj.shape[1] - 2 * states
    slot = page_table % state_pool.shape[0]
    peers = lax.axis_size("dp")

    full = lax.all_gather(hidden, "mp", axis=2, tiled=True)
    gain = lax.all_gather(norm_gain, "mp", axis=0, tiled=True)
    x_weight = lax.all_gather(in_x, "dp", axis=0, tiled=True)
    z_weight = lax.all_gather(in_z, "dp", axis=0, tiled=True)
    x_proj = lax.all_gather(x_proj, "dp", axis=0, tiled=True)
    dt_proj = lax.all_gather(dt_proj, "dp", axis=0, tiled=True)
    out_proj = lax.all_gather(out_proj, "dp", axis=1, tiled=True)

    rows = full.reshape(tokens, -1).astype(jnp.float32)
    scale = lax.rsqrt(jnp.mean(rows * rows, axis=1, keepdims=True) + EPS)
    normed = (rows * scale * gain.astype(jnp.float32)).astype(jnp.bfloat16)
    x_part = jnp.dot(normed, x_weight, preferred_element_type=jnp.float32).astype(jnp.bfloat16)
    z_part = jnp.dot(normed, z_weight, preferred_element_type=jnp.float32).astype(jnp.bfloat16)
    x_part = x_part.reshape(count, drafts, inner_local)
    z_part = z_part.reshape(count, drafts, inner_local)

    inputs, partial, new_conv_pool = conv_branch(
        x_part, conv_pool, conv_weight, conv_bias, x_proj, slot, accepted
    )
    summed = lax.psum(partial, "mp")
    low = summed[:, :rank].astype(jnp.bfloat16).reshape(count, drafts, rank)
    both = summed[:, rank:].reshape(count, drafts, 2 * states).transpose(0, 2, 1)
    gated, new_state_pool = scan_branch(
        low, dt_proj, dt_bias, a_log, skip, inputs, z_part, both, state_pool, slot, accepted
    )
    terms = jnp.dot(gated.reshape(tokens, inner_local), out_proj, preferred_element_type=jnp.float32)
    layer = lax.psum_scatter(terms, "mp", scatter_dimension=1, tiled=True)
    layer = (layer + hidden.reshape(tokens, width_local).astype(jnp.float32)).astype(jnp.bfloat16)
    verified = route(layer.reshape(count, drafts, width_local), permutation, count, peers)
    return (verified, new_state_pool, new_conv_pool)


def solution(mesh):
    return jax.shard_map(
        on_device,
        mesh=mesh,
        in_specs=(
            P("dp", None, "mp"),
            P("mp"),
            P("dp", "mp"),
            P("dp", "mp"),
            P(None, "mp"),
            P("mp"),
            P(("mp", "dp"), None),
            P("dp", "mp"),
            P("mp"),
            P(None, "mp"),
            P("mp"),
            P("mp", "dp"),
            P("dp", None, "mp"),
            P("dp", None, "mp"),
            P("dp"),
            P("dp"),
            P("dp"),
        ),
        out_specs=(P("dp", None, "mp"), P("dp", None, "mp"), P("dp", None, "mp")),
        check_vma=False,
    )
```

time: 388 us -> 325 us (0.84)
  waiting for transfers between devices: 77.6 us -> 203 us
  local copies, waits for them, and re-layouts: 89.1 us -> 11.2 us
  other arithmetic: 85.6 us -> 9.33 us
  blocking collectives: 71.1 us -> 32.2 us
  Pallas kernels: 0 us -> 27.9 us
  starting transfers between devices: 22.7 us -> 4.52 us
    all_gather x4, waiting for transfers between devices: 11.4 us -> 86 us  [the longest x1 34.1 us: on_device(): x_weight = lax.all_gather(in_x, 'dp', axis=0, tiled=True)]
    reduce_scatter x1, waiting for transfers between devices: 26.1 us -> 75.2 us  [on_device(): layer = lax.psum_scatter(terms, 'mp', scatter_dimension=1, tiled=True)]
    pallas_call x0 -> x2, Pallas kernels: none -> 27.9 us  [the longest x1 23.5 us: scan_branch(): pl.pallas_call(scan_kernel, out_shape=(jax.ShapeDtypeStruct(inputs.shape,...]
    mul x32 -> x0, local copies, waits for them, and re-layouts: 27.8 us -> none  [the longest x16 15.9 us: advance(): step_drive[:, None, :] * step_b[:, :, None]]
    gather x16 -> x2, local copies, waits for them, and re-layouts: 26.3 us -> 1.16 us  [the longest x1 0.58 us: route(): sent = jnp.take(grouped, klass, axis=0)]
    all_gather x3, blocking collectives: 52.7 us -> 32.2 us  [the longest x1 12.9 us: on_device(): x_proj = lax.all_gather(x_proj, 'dp', axis=0, tiled=True)]
    reduce_sum x18 -> x1, other arithmetic: 22.1 us -> 2.05 us  [on_device(): scale = lax.rsqrt(jnp.mean(rows * rows, axis=1, keepdims=True) + EPS)]
    psum x1, waiting for transfers between devices: 13.4 us -> 33.2 us  [on_device(): summed = lax.psum(partial, 'mp')]
  transfers between devices with their start and end apart: 10 -> 7, of which waited for: 6 -> 7; matrix products, arithmetic and copies ran while one was open for 46% -> 8% of each run, Pallas kernels for 0% -> 9%
where the time goes in v1:
time: 325 us; the launch traced here: 320 us
  waiting for transfers between devices  203 us (62%)
  blocking collectives  32.2 us (10%)
  Pallas kernels  27.9 us (9%)
  matrix products  18.2 us (6%)
  between operations  14.3 us (4%)
  local copies, waits for them, and re-layouts  11.2 us (3%)
  other arithmetic  9.33 us (3%)
  starting transfers between devices  4.52 us (1%)
    reduce_scatter x1, waiting for transfers between devices, on_device(): layer = lax.psum_scatter(terms, 'mp', scatter_dimension=1, tiled=True)  75.2 us
    all_gather x1, waiting for transfers between devices, on_device(): x_weight = lax.all_gather(in_x, 'dp', axis=0, tiled=True)  34.1 us
    psum x1, waiting for transfers between devices, on_device(): summed = lax.psum(partial, 'mp')  33.2 us
    pallas_call x1, Pallas kernels, scan_branch(): pl.pallas_call(scan_kernel, out_shape=(jax.ShapeDtypeStruct(inputs.shape,...  23.5 us
    all_gather x1, waiting for transfers between devices, on_device(): z_weight = lax.all_gather(in_z, 'dp', axis=0, tiled=True)  19.7 us
    all_gather x1, waiting for transfers between devices, on_device(): full = lax.all_gather(hidden, 'mp', axis=2, tiled=True)  19.3 us
    all_gather x1, blocking collectives, on_device(): x_proj = lax.all_gather(x_proj, 'dp', axis=0, tiled=True)  12.9 us
    all_gather x1, waiting for transfers between devices, on_device(): out_proj = lax.all_gather(out_proj, 'dp', axis=1, tiled=True)  12.9 us
  transfers between devices with their start and end apart: 7, of which 7 were waited for; matrix products, arithmetic and copies ran while one was open for 8% of the time, Pallas kernels for 9%

profile of v1, /device:TPU:9, one launch (start us, length us, event | category | flops | bytes accessed | tf_op | source)
XLA Modules:
  0.0 320.2 jit_solution(3043192357537803986)
XLA Ops:
  7.2 0.0 all-gather.6.cloned.1.call-start
  7.2 0.7 all-gather.6.cloned.1.call-update
  7.9 0.0 all-gather.8.cloned.1.call-start
  7.9 0.7 all-gather.8.cloned.1.call-update
  8.6 0.0 all-gather.10.cloned.1.call-start
  8.7 0.7 all-gather.10.cloned.1.call-update
  9.4 0.0 all-reduce.2.cloned.1.call-start
  9.4 0.7 reshape.99
  10.1 9.5 %all-gather = bf16[4,1,512]{2,1,0:T(2,128)(2,1)S(1)} all-gather(bf16[1,1,512]{2,1,0:T(2,128)(2,1)S(1)} %reshape.99), channel_id=1, replica_groups=mesh['dp'=8,'mp'=4] {'mp'}, dimensions={0}, use_global_device_ids=true | all-gather | bytes 5120 | tf_op jit(solution)/shard_map/all_gather | solution.py:157
  19.6 1.4 copy.35.pool_ref
  21.0 0.9 copy.34
  21.9 12.9 %all_gather.24.proj_ref = bf16[1024,160]{1,0:T(8,128)(2,1)S(1)} all-gather(bf16[128,160]{1,0:T(8,128)(2,1)S(1)} %copy.34), channel_id=1, replica_groups=mesh['dp'=8,'mp'=4] {'dp'}, dimensions={0}, use_global_device_ids=true | all-gather | bytes 368640 | tf_op jit(solution)/shard_map/all_gather | solution.py:160
  34.9 0.7 and_select_fusion.4.slot_ref
  35.5 19.3 %all-gather.6.cloned.1.call-done = bf16[32,16,2048]{2,1,0:T(8,128)(2,1)} async-done(((bf16[32,16,512]{2,1,0:T(8,128)(2,1)}), bf16[32,16,2048]{2,1,0:T(8,128)(2,1)}) %all-gather.6.cloned.1.call-update) | async-done | bytes 2097168 | tf_op jit(solution)/shard_map/all_gather | solution.py:156
  54.8 2.1 multiply_reduce_fusion
  56.9 0.1 rsqrt.12
  57.0 3.5 %fusion.1 = bf16[512,2048]{1,0:T(8,128)(2,1)} fusion(f32[2048]{0:T(1024)S(1)} %bitcast.42, f32[512]{0:T(512)S(1)} %rsqrt.12, bf16[32,16,2048]{2,1,0:T(8,128)(2,1)} %all-gather.6.cloned.1.call-done), kind=kLoop, calls=%fused_computation.4 | loop fusion | flops 4194304 | bytes 4204544 | tf_op jit(solution)/shard_map/convert_element_type | solution.py:166
  60.5 34.1 %all-gather.8.cloned.1.call-done = bf16[2048,1024]{1,0:T(8,128)(2,1)} async-done(((bf16[256,1024]{1,0:T(8,128)(2,1)}), bf16[2048,1024]{1,0:T(8,128)(2,1)}) %all-gather.8.cloned.1.call-update) | async-done | bytes 4194320 | tf_op jit(solution)/shard_map/all_gather | solution.py:158
  94.5 5.2 %convolution_convert_fusion.1 = bf16[512,1024]{1,0:T(8,128)(2,1)S(1)} fusion(bf16[512,2048]{1,0:T(8,128)(2,1)} %fusion.1, bf16[2048,1024]{1,0:T(8,128)(2,1)} %all-gather.8.cloned.1.call-done), kind=kOutput, calls=%fused_computation.7 | convolution fusion | flops 2148007936 | bytes 7340032 | tf_op jit(solution)/shard_map/dot_general | solution.py:167
  99.7 4.4 %shard_map.184 = (bf16[32,16,1024]{2,1,0:T(8,128)(2,1)S(1)}, f32[512,160]{1,0:T(8,128)}, f32[40,3,1024]{2,1,0:T(4,128)S(1)}) custom-call(s32[32]{0:T(128)S(1)} %and_select_fusion.4.slot_ref, s32[32]{0:T(128)S(1)} %copy-done.2, bf16[32,16,1024]{2,1,0:T(8,128)(2,1)S(1)} %bitcast.31, f32[40,3,1024]{2,1,0:T(4,128)S(1)} %copy.35.pool_ref, f32[4,1024]{1,0:T(4,128)S(1)} %copy-done, ...), custom_call_target="tpu_custom_call" | custom-call | flops 200000000 | bytes 4000000 | tf_op jit(solution)/shard_map/pallas_call | solution.py:47
  104.1 0.0 all-reduce.2.cloned.1.call-update
  104.1 0.0 all-gather.12.cloned.1.call-start
  104.2 0.5 all-gather.12.cloned.1.call-update
  104.7 0.0 reduce-scatter.2.cloned.1.call-start
  104.8 9.8 %all_gather.25.proj_ref = bf16[128,1024]{1,0:T(8,128)(2,1)S(1)} all-gather(bf16[16,1024]{1,0:T(8,128)(2,1)S(1)} %copy-done.9), channel_id=1, replica_groups=mesh['dp'=8,'mp'=4] {'dp'}, dimensions={0}, use_global_device_ids=true | all-gather | bytes 294912 | tf_op jit(solution)/shard_map/all_gather | solution.py:161
  114.6 19.7 %all-gather.10.cloned.1.call-done = bf16[2048,1024]{1,0:T(8,128)(2,1)} async-done(((bf16[256,1024]{1,0:T(8,128)(2,1)}), bf16[2048,1024]{1,0:T(8,128)(2,1)}) %all-gather.10.cloned.1.call-update) | async-done | bytes 4194320 | tf_op jit(solution)/shard_map/all_gather | solution.py:159
  134.2 6.2 %convolution_convert_fusion = bf16[512,1024]{1,0:T(8,128)(2,1)} fusion(bf16[512,2048]{1,0:T(8,128)(2,1)} %fusion.1, bf16[2048,1024]{1,0:T(8,128)(2,1)} %all-gather.10.cloned.1.call-done), kind=kOutput, calls=%fused_computation.6 | convolution fusion | flops 2148007936 | bytes 7340032 | tf_op jit(solution)/shard_map/dot_general | solution.py:168
  140.5 33.2 %all-reduce.2.cloned.1.call-done = f32[512,160]{1,0:T(8,128)} async-done(((f32[512,160]{1,0:T(8,128)}), f32[512,160]{1,0:T(8,128)}) %all-reduce.2.cloned.1.call-update) | async-done | bytes 327696 | tf_op jit(solution)/shard_map/psum | solution.py:175
  173.6 1.0 slice.18
  174.6 0.2 copy.36
  174.8 1.0 slice.21
  175.8 1.2 copy-done.6
  177.1 23.5 %shard_map.185 = (bf16[32,16,1024]{2,1,0:T(8,128)(2,1)S(1)}, f32[40,16,1024]{2,1,0:T(8,128)}) custom-call(s32[32]{0:T(128)S(1)} %and_select_fusion.4.slot_ref, s32[32]{0:T(128)S(1)} %copy-done.2, bf16[32,16,128]{2,1,0:T(8,128)(2,1)S(1)} %bitcast.33, bf16[128,1024]{1,0:T(8,128)(2,1)S(1)} %all_gather.25.proj_ref, f32[1,1024]{1,0:T(1,128)S(1)} %bitcast.35, ...), custom_call_target="tpu_custom_call" | custom-call | flops 100000000 | bytes 10000000 | tf_op jit(solution)/shard_map/pallas_call | solution.py:106
  200.6 1.1 copy-done.7
  201.6 12.9 %all-gather.12.cloned.1.call-done = bf16[1024,2048]{1,0:T(8,128)(2,1)} async-done(((bf16[1024,256]{1,0:T(8,128)(2,1)}), bf16[1024,2048]{1,0:T(8,128)(2,1)}) %all-gather.12.cloned.1.call-update) | async-done | bytes 4194320 | tf_op jit(solution)/shard_map/all_gather | solution.py:162
  214.6 6.8 %fusion.6 = f32[512,2048]{1,0:T(8,128)} fusion(bf16[512,1024]{1,0:T(8,128)(2,1)} %bitcast.38, bf16[1024,2048]{1,0:T(8,128)(2,1)} %all-gather.12.cloned.1.call-done), kind=kOutput, calls=%fused_computation.39 | convolution fusion | flops 2147483648 | bytes 9437184 | tf_op jit(solution)/shard_map/dot_general | solution.py:181
  221.4 0.6 copy-done.10
  222.1 0.6 iota_reduce_fusion
  222.7 75.2 %reduce-scatter.2.cloned.1.call-done = f32[512,512]{1,0:T(8,128)} async-done(((f32[512,2048]{1,0:T(8,128)}), f32[512,512]{1,0:T(8,128)}) %reduce-scatter.2.cloned.1.call-update) | async-done | bytes 1048592 | tf_op jit(solution)/shard_map/reduce_scatter | solution.py:182
  297.9 1.4 fusion.2
  299.3 0.6 gather_fusion
  299.9 0.9 broadcast_select_fusion
  300.8 4.3 %all-to-all-start = ((bf16[8,4,16,512]{3,2,1,0:T(8,128)(2,1)}), bf16[8,4,16,512]{3,2,1,0:T(8,128)(2,1)S(1)}, u32[]{:S(2)}, u32[]{:S(2)}) async-start(bf16[8,4,16,512]{3,2,1,0:T(8,128)(2,1)} %broadcast_select_fusion), calls=%async_computation.1 | async-start | bytes 1048576 | tf_op jit(solution)/shard_map/all_to_all | solution.py:138
  305.1 1.1 copy.38
  306.2 5.7 %all-to-all-done = bf16[8,4,16,512]{3,2,1,0:T(8,128)(2,1)S(1)} async-done(((bf16[8,4,16,512]{3,2,1,0:T(8,128)(2,1)}), bf16[8,4,16,512]{3,2,1,0:T(8,128)(2,1)S(1)}, u32[]{:S(2)}, u32[]{:S(2)}) %all-to-all-start) | async-done | bytes 524320 | tf_op jit(solution)/shard_map/all_to_all | solution.py:138
  311.8 0.6 gather_fusion.1
  312.4 0.1 select_bitcast_fusion
  312.5 0.8 copy.37
  (28 shorter events, 0.2 us)
Async XLA Ops:
  7.2 47.7 %all-gather.6.cloned.1.call-start = ((), (), s32[]{:S(2)}) async-start(), calls=%async_computation.2 | async-start | bytes 2621440 | tf_op jit(solution)/shard_map/all_gather | solution.py:156
  7.9 86.6 %all-gather.8.cloned.1.call-start = ((), (), s32[]{:S(2)}) async-start(), calls=%async_computation.3 | async-start | bytes 4718592 | tf_op jit(solution)/shard_map/all_gather | solution.py:158
  8.6 125.6 %all-gather.10.cloned.1.call-start = ((), (), s32[]{:S(2)}) async-start(), calls=%async_computation.5 | async-start | bytes 4718592 | tf_op jit(solution)/shard_map/all_gather | solution.py:159
  9.4 164.2 %all-reduce.2.cloned.1.call-start = ((), (), s32[]{:S(2)}) async-start(), calls=%async_computation.4 | async-start | bytes 1048576 | tf_op jit(solution)/shard_map/psum | solution.py:175
  60.5 39.2 %copy-start = (f32[4,1024]{1,0:T(4,128)S(1)}, f32[4,1024]{1,0:T(4,128)}, u32[]{:S(2)}) copy-start(f32[4,1024]{1,0:T(4,128)} %weight_ref.1) | copy-start | bytes 49156
  60.5 39.2 %copy-start.1 = (f32[1024]{0:T(1024)S(1)}, f32[1024]{0:T(1024)}, u32[]{:S(2)}) copy-start(f32[1024]{0:T(1024)} %param.24) | copy-start | bytes 12292
  60.5 39.2 %copy-start.2 = (s32[32]{0:T(128)S(1)}, s32[32]{0:T(128)}, u32[]{:S(2)}) copy-start(s32[32]{0:T(128)} %accepted_ref.3) | copy-start | bytes 388
  60.5 44.3 %copy-start.9 = (bf16[16,1024]{1,0:T(8,128)(2,1)S(1)}, bf16[16,1024]{1,0:T(8,128)(2,1)}, u32[]{:S(2)}) copy-start(bf16[16,1024]{1,0:T(8,128)(2,1)} %param.26) | copy-start | bytes 98308
  104.1 110.4 %all-gather.12.cloned.1.call-start = ((), (), s32[]{:S(2)}) async-start(), calls=%async_computation.6 | async-start | bytes 4718592 | tf_op jit(solution)/shard_map/all_gather | solution.py:162
  104.7 193.2 %reduce-scatter.2.cloned.1.call-start = ((), (), s32[]{:S(2)}) async-start(), calls=%async_computation.7 | async-start | bytes 5242880 | tf_op jit(solution)/shard_map/reduce_scatter | solution.py:182
  114.6 61.2 %copy-start.3 = (f32[16,1024]{1,0:T(8,128)S(1)}, f32[16,1024]{1,0:T(8,128)}, u32[]{:S(2)}) copy-start(f32[16,1024]{1,0:T(8,128)} %a_log_ref.1) | copy-start | bytes 196612
  114.6 61.2 %copy-start.4 = (f32[1024]{0:T(1024)S(1)}, f32[1024]{0:T(1024)}, u32[]{:S(2)}) copy-start(f32[1024]{0:T(1024)} %param.27) | copy-start | bytes 12292
  114.6 61.3 %copy-start.5 = (f32[1024]{0:T(1024)S(1)}, f32[1024]{0:T(1024)}, u32[]{:S(2)}) copy-start(f32[1024]{0:T(1024)} %param.29) | copy-start | bytes 12292
  175.8 1.2 copy-start.6
  200.6 1.1 copy-start.7
  221.4 0.7 copy-start.10
  221.4 76.5 %copy-start.8 = (bf16[32,16,512]{2,1,0:T(8,128)(2,1)S(1)}, bf16[32,16,512]{2,1,0:T(8,128)(2,1)}, u32[]{:S(2)}) copy-start(bf16[32,16,512]{2,1,0:T(8,128)(2,1)} %param.19) | copy-start | bytes 1572868
  300.8 11.0 %all-to-all-start = ((bf16[8,4,16,512]{3,2,1,0:T(8,128)(2,1)}), bf16[8,4,16,512]{3,2,1,0:T(8,128)(2,1)S(1)}, u32[]{:S(2)}, u32[]{:S(2)}) async-start(bf16[8,4,16,512]{3,2,1,0:T(8,128)(2,1)} %broadcast_select_fusion), calls=%async_computation.1 | async-start | bytes 1048576 | tf_op jit(solution)/shard_map/all_to_all | solution.py:138
Sparse Core Ops, SparseCore 0:
  9.6 45.2 all-gather.5
  56.7 37.7 all-gather.7
  96.4 37.7 all-gather.9
  137.0 36.5 all-reduce.1
  175.4 39.1 all-gather.11
  221.5 76.3 reduce-scatter.1

commit v2 on v1

--- a/solution.py
+++ b/solution.py
@@ -125,20 +125,305 @@
     )
 
 
-def route(rows, permutation, count, peers):
-    period = min(count, peers)
+MESH = pl.DeviceIdType.MESH
+
+
+def greet(partners):
+    barrier = pltpu.get_barrier_semaphore()
+    for partner in partners:
+        pl.semaphore_signal(barrier, inc=1, device_id=partner, device_id_type=MESH)
+    pl.semaphore_wait(barrier, len(partners))
+
+
+def peers_on(axis, size):
+    me = lax.axis_index(axis)
+    return [{axis: lax.rem(me + k, size)} for k in range(1, size)]
+
+
+def gather_kernel(n_mp, n_dp, *refs):
+    weights = 4 if n_dp == 8 else 0
+    hidden, gain = refs[0], refs[1]
+    shards = refs[2 : 2 + weights]
+    full, gains = refs[2 + weights], refs[3 + weights]
+    wholes = refs[4 + weights : 4 + 2 * weights]
+    send, recv, local = refs[4 + 2 * weights :]
+    m = lax.axis_index("mp")
+    width = hidden.shape[1]
+    greet(peers_on("mp", n_mp) + (peers_on("dp", n_dp) if weights else []))
+    made = []
+
+    def remote(src, dst, target):
+        index = len(made)
+        copy = pltpu.make_async_remote_copy(
+            src_ref=src, dst_ref=dst, send_sem=send.at[index], recv_sem=recv.at[index],
+            device_id=target, device_id_type=MESH,
+        )
+        made.append(copy)
+        return copy
+
+    def started(src, dst, target):
+        copy = remote(src, dst, target)
+        copy.start()
+        return copy
+
+    def place(origin):
+        start = pl.multiple_of(jnp.clip(origin, 0, n_mp - 1) * width, width)
+        return full.at[:, pl.ds(start, width)]
+
+    kept = []
+
+    def keep(src, dst):
+        copy = pltpu.make_async_copy(src, dst, local.at[len(kept)])
+        copy.start()
+        kept.append(copy)
+
+    right, left = jnp.minimum(m + 1, n_mp - 1), jnp.maximum(m - 1, 0)
+    steps = n_mp - 1
+    relay = []
+    for s in range(steps):
+        src = hidden if s == 0 else place(m - s)
+        ahead = remote(src, place(m - s), {"mp": right})
+        src = hidden if s == 0 else place(m + s)
+        back = remote(src, place(m + s), {"mp": left})
+        relay.append((ahead, back))
+    relayed = len(made)
+
+    def sends(s):
+        return (m - s >= 0) & (m + 1 < n_mp), (m + s < n_mp) & (m >= 1)
+
+    def gets(s):
+        return m - 1 - s >= 0, m + 1 + s < n_mp
+
+    def relay_start(s):
+        for copy, go in zip(relay[s], sends(s)):
+            pl.when(go)(copy.start)
+
+    def relay_arrive(s):
+        for copy, go in zip(relay[s], gets(s)):
+            pl.when(go)(copy.wait_recv)
+
+    relay_start(0)
+    keep(hidden, place(m))
+    keep(gain, gains.at[m])
+    if weights:
+        d = lax.axis_index("dp")
+        other = lambda bit: d + bit - 2 * bit * lax.rem(d // bit, 2)
+        core, by_x, by_y = other(1), other(2), other(4)
+        diagonal = by_x + 4 - 8 * lax.rem(d // 4, 2)
+        own = []
+        for w in range(2):
+            shard, whole_w = shards[w], wholes[w]
+            own.append([started(shard, whole_w.at[d], {"dp": t}) for t in (by_x, by_y, core)])
+            keep(shard, whole_w.at[d])
+    for k in range(1, n_mp):
+        started(gain, gains.at[m], {"mp": lax.rem(m + k, n_mp)})
+    if weights:
+        for w in range(2, 4):
+            keep(shards[w], wholes[w].at[d])
+            for k in range(1, n_dp):
+                started(shards[w], wholes[w].at[d], {"dp": lax.rem(d + k, n_dp)})
+    relay_arrive(0)
+    relay_start(1)
+    done = {id(copy) for pair in relay for copy in pair}
+
+    def arrive(copy):
+        copy.wait_recv()
+        done.add(id(copy))
+
+    if weights:
+        halves = []
+        for w in range(2):
+            whole_w = wholes[w]
+            half = whole_w.shape[1] // 2
+            low, high = pl.ds(0, half), pl.ds(half, half)
+            arrive(own[w][0])
+            first = started(whole_w.at[by_x, low], whole_w.at[by_x, low], {"dp": by_y})
+            started(whole_w.at[by_x], whole_w.at[by_x], {"dp": core})
+            arrive(own[w][1])
+            second = started(whole_w.at[by_y, high], whole_w.at[by_y, high], {"dp": by_x})
+            started(whole_w.at[by_y], whole_w.at[by_y], {"dp": core})
+            halves.append((first, second))
+            if w == 0:
+                relay_arrive(1)
+                relay_start(2)
+        for w in range(2):
+            whole_w = wholes[w]
+            half = whole_w.shape[1] // 2
+            for copy, part in zip(halves[w], (pl.ds(0, half), pl.ds(half, half))):
+                arrive(copy)
+                started(whole_w.at[diagonal, part], whole_w.at[diagonal, part], {"dp": core})
+    else:
+        relay_arrive(1)
+        relay_start(2)
+    relay_arrive(2)
+    for copy in made:
+        if id(copy) not in done:
+            copy.wait_recv()
+    for s in range(steps):
+        for copy, go in zip(relay[s], sends(s)):
+            pl.when(go)(copy.wait_send)
+    for copy in made[relayed:]:
+        copy.wait_send()
+    for copy in kept:
+        copy.wait()
+
+
+def gather(hidden, gain, weights, n_mp, n_dp):
+    tokens, width = hidden.shape
+    gain = jnp.broadcast_to(gain[None, :], (16, width))
+    shapes = [(tokens, n_mp * width), (n_mp, 16, width)] + [(n_dp,) + w.shape for w in weights]
+    anywhere = pl.BlockSpec(memory_space=pl.ANY)
+    copies = 2 * (n_mp - 1) + n_mp - 1 + (2 * (3 + 4 + 2) + 2 * (n_dp - 1) if weights else 0)
+    return pl.pallas_call(
+        functools.partial(gather_kernel, n_mp, n_dp),
+        out_shape=tuple(jax.ShapeDtypeStruct(s, jnp.bfloat16) for s in shapes),
+        in_specs=[anywhere] * (2 + len(weights)),
+        out_specs=tuple([anywhere] * len(shapes)),
+        scratch_shapes=[
+            pltpu.SemaphoreType.DMA((copies,)),
+            pltpu.SemaphoreType.DMA((copies,)),
+            pltpu.SemaphoreType.DMA((2 + len(weights),)),
+        ],
+        compiler_params=pltpu.CompilerParams(collective_id=0, has_side_effects=True),
+        cost_estimate=pl.CostEstimate(flops=0, bytes_accessed=100_000_000, transcendentals=0),
+    )(hidden, gain, *weights)
+
+
+def sum_kernel(n_mp, partial_ref, total_ref, sent, landed, send, recv):
+    m = lax.axis_index("mp")
+    rows = partial_ref.shape[0] // n_mp
+    greet(peers_on("mp", n_mp))
+    copies = []
+    for k in range(1, n_mp):
+        target = lax.rem(m + k, n_mp)
+        piece = partial_ref[pl.ds(pl.multiple_of(target * rows, rows), rows), :]
+        sent[k - 1] = piece.astype(jnp.bfloat16)
+        copy = pltpu.make_async_remote_copy(
+            src_ref=sent.at[k - 1], dst_ref=landed.at[k - 1], send_sem=send.at[k - 1],
+            recv_sem=recv.at[k - 1], device_id={"mp": target}, device_id_type=MESH,
+        )
+        copy.start()
+        copies.append(copy)
+    mine = pl.ds(pl.multiple_of(m * rows, rows), rows)
+    total = partial_ref[mine, :]
+    for k in range(1, n_mp):
+        copies[k - 1].wait_recv()
+        total = total + landed[k - 1].astype(jnp.float32)
+    total_ref[mine, :] = total.astype(jnp.bfloat16)
+    spread = []
+    for k in range(1, n_mp):
+        copy = pltpu.make_async_remote_copy(
+            src_ref=total_ref.at[mine], dst_ref=total_ref.at[mine],
+            send_sem=send.at[n_mp - 2 + k], recv_sem=recv.at[n_mp - 2 + k],
+            device_id={"mp": lax.rem(m + k, n_mp)}, device_id_type=MESH,
+        )
+        copy.start()
+        spread.append(copy)
+    for copy in spread:
+        copy.wait_recv()
+    for copy in copies + spread:
+        copy.wait_send()
+
+
+def sum_over_mp(partial, n_mp):
+    rows, columns = partial.shape
+    return pl.pallas_call(
+        functools.partial(sum_kernel, n_mp),
+        out_shape=jax.ShapeDtypeStruct(partial.shape, jnp.bfloat16),
+        in_specs=whole(1),
+        out_specs=whole(1)[0],
+        scratch_shapes=[
+            pltpu.VMEM((n_mp - 1, rows // n_mp, columns), jnp.bfloat16),
+            pltpu.VMEM((n_mp - 1, rows // n_mp, columns), jnp.bfloat16),
+            pltpu.SemaphoreType.DMA((2 * (n_mp - 1),)),
+            pltpu.SemaphoreType.DMA((2 * (n_mp - 1),)),
+        ],
+        compiler_params=pltpu.CompilerParams(collective_id=1, has_side_effects=True),
+        cost_estimate=pl.CostEstimate(flops=0, bytes_accessed=20_000_000, transcendentals=0),
+    )(partial)
+
+
+def output_kernel(
+    n_mp, n_dp, shift_ref, class_ref, gated_ref, proj_ref, hidden_ref, out_ref,
+    sent, landed, total, rows, outgoing, incoming, send, recv,
+):
+    m, d = lax.axis_index("mp"), lax.axis_index("dp")
+    width = hidden_ref.shape[1]
+    capacity, period, drafts, _ = rows.shape
+    greet(peers_on("mp", n_mp) + peers_on("dp", n_dp))
+
+    def share(target):
+        columns = pl.ds(pl.multiple_of(target * width, width), width)
+        return jnp.dot(gated_ref[...], proj_ref[:, columns], preferred_element_type=jnp.float32)
+
+    copies = []
+    for k in range(1, n_mp):
+        target = lax.rem(m + k, n_mp)
+        sent[k - 1] = share(target).astype(jnp.bfloat16)
+        copy = pltpu.make_async_remote_copy(
+            src_ref=sent.at[k - 1], dst_ref=landed.at[k - 1], send_sem=send.at[k - 1],
+            recv_sem=recv.at[k - 1], device_id={"mp": target}, device_id_type=MESH,
+        )
+        copy.start()
+        copies.append(copy)
+    total[...] = share(m) + hidden_ref[...].astype(jnp.float32)
+    for copy in copies:
+        copy.wait_recv()
+    layer = total[...]
+    for k in range(1, n_mp):
+        layer = layer + landed[k - 1].astype(jnp.float32)
+    rows[...] = layer.astype(jnp.bfloat16).reshape(rows.shape)
+    for o in range(n_dp):
+        for c in range(capacity):
+            outgoing[o, c] = rows[c, class_ref[o]]
+        if o == 0:
+            incoming[0] = outgoing[0]
+            continue
+        index = n_mp - 2 + o
+        copy = pltpu.make_async_remote_copy(
+            src_ref=outgoing.at[o], dst_ref=incoming.at[o], send_sem=send.at[index],
+            recv_sem=recv.at[index], device_id={"dp": lax.rem(d + o, n_dp)}, device_id_type=MESH,
+        )
+        copy.start()
+        copies.append(copy)
+    for copy in copies[n_mp - 1 :]:
+        copy.wait_recv()
+    for k in range(period):
+        for c in range(capacity):
+            out_ref[c * period + k] = incoming[shift_ref[k], c]
+    for copy in copies:
+        copy.wait_send()
+
+
+def output_branch(gated, out_proj, hidden, permutation, count, n_mp, n_dp):
+    tokens, width = hidden.shape
+    drafts = tokens // count
+    period = min(count, n_dp)
     capacity = count // period
-    me = lax.axis_index("dp")
-    shift = (permutation[:period] // count - me + peers) % peers
-    chunks = jnp.arange(peers)
-    hit = chunks[:, None] == (me + shift[None, :]) % peers
-    klass = jnp.argmax(hit, axis=1)
-    grouped = rows.reshape((capacity, period) + rows.shape[1:]).swapaxes(0, 1)
-    sent = jnp.take(grouped, klass, axis=0)
-    got = lax.all_to_all(sent, "dp", split_axis=0, concat_axis=0, tiled=True)
-    source = (me - shift + peers) % peers
-    placed = jnp.take(got, source, axis=0)
-    return placed.swapaxes(0, 1).reshape(rows.shape)
+    shift = (permutation[:period] // count - lax.axis_index("dp") + n_dp) % n_dp
+    klass = jnp.argmax(jnp.arange(n_dp)[:, None] == shift[None, :], axis=1).astype(jnp.int32)
+    box = (n_dp, capacity, drafts, width)
+    copies = n_mp - 1 + n_dp - 1
+    return pl.pallas_call(
+        functools.partial(output_kernel, n_mp, n_dp),
+        out_shape=jax.ShapeDtypeStruct((count, drafts, width), jnp.bfloat16),
+        in_specs=whole(5, smem=2),
+        out_specs=whole(1)[0],
+        scratch_shapes=[
+            pltpu.VMEM((n_mp - 1, tokens, width), jnp.bfloat16),
+            pltpu.VMEM((n_mp - 1, tokens, width), jnp.bfloat16),
+            pltpu.VMEM((tokens, width), jnp.float32),
+            pltpu.VMEM((capacity, period, drafts, width), jnp.bfloat16),
+            pltpu.VMEM(box, jnp.bfloat16),
+            pltpu.VMEM(box, jnp.bfloat16),
+            pltpu.SemaphoreType.DMA((copies,)),
+            pltpu.SemaphoreType.DMA((copies,)),
+        ],
+        compiler_params=pltpu.CompilerParams(
+            collective_id=2, has_side_effects=True, vmem_limit_bytes=VMEM_BYTES
+        ),
+        cost_estimate=pl.CostEstimate(flops=2_000_000_000, bytes_accessed=100_000_000, transcendentals=0),
+    )(shift.astype(jnp.int32), klass, gated, out_proj, hidden)
 
 
 def on_device(
@@ -151,17 +436,22 @@
     states = a_log.shape[0]
     rank = x_proj.shape[1] - 2 * states
     slot = page_table % state_pool.shape[0]
-    peers = lax.axis_size("dp")
-
-    full = lax.all_gather(hidden, "mp", axis=2, tiled=True)
-    gain = lax.all_gather(norm_gain, "mp", axis=0, tiled=True)
-    x_weight = lax.all_gather(in_x, "dp", axis=0, tiled=True)
-    z_weight = lax.all_gather(in_z, "dp", axis=0, tiled=True)
-    x_proj = lax.all_gather(x_proj, "dp", axis=0, tiled=True)
-    dt_proj = lax.all_gather(dt_proj, "dp", axis=0, tiled=True)
+    n_dp, n_mp = lax.axis_size("dp"), lax.axis_size("mp")
+    flat_hidden = hidden.reshape(tokens, width_local)
+
     out_proj = lax.all_gather(out_proj, "dp", axis=1, tiled=True)
-
-    rows = full.reshape(tokens, -1).astype(jnp.float32)
+    if n_dp == 8:
+        weights = (in_x, in_z, x_proj, dt_proj)
+        full, gain, *weights = gather(flat_hidden, norm_gain, weights, n_mp, n_dp)
+        x_weight, z_weight, x_proj, dt_proj = [w.reshape(-1, w.shape[2]) for w in weights]
+    else:
+        full, gain = gather(flat_hidden, norm_gain, (), n_mp, n_dp)
+        x_weight, z_weight, x_proj, dt_proj = [
+            lax.all_gather(w, "dp", axis=0, tiled=True) for w in (in_x, in_z, x_proj, dt_proj)
+        ]
+    gain = gain[:, 0, :].reshape(-1)
+
+    rows = full.astype(jnp.float32)
     scale = lax.rsqrt(jnp.mean(rows * rows, axis=1, keepdims=True) + EPS)
     normed = (rows * scale * gain.astype(jnp.float32)).astype(jnp.bfloat16)
     x_part = jnp.dot(normed, x_weight, preferred_element_type=jnp.float32).astype(jnp.bfloat16)
@@ -172,16 +462,15 @@
     inputs, partial, new_conv_pool = conv_branch(
         x_part, conv_pool, conv_weight, conv_bias, x_proj, slot, accepted
     )
-    summed = lax.psum(partial, "mp")
-    low = summed[:, :rank].astype(jnp.bfloat16).reshape(count, drafts, rank)
-    both = summed[:, rank:].reshape(count, drafts, 2 * states).transpose(0, 2, 1)
+    summed = sum_over_mp(partial, n_mp)
+    low = summed[:, :rank].reshape(count, drafts, rank)
+    both = summed[:, rank:].astype(jnp.float32).reshape(count, drafts, 2 * states).transpose(0, 2, 1)
     gated, new_state_pool = scan_branch(
         low, dt_proj, dt_bias, a_log, skip, inputs, z_part, both, state_pool, slot, accepted
     )
-    terms = jnp.dot(gated.reshape(tokens, inner_local), out_proj, preferred_element_type=jnp.float32)
-    layer = lax.psum_scatter(terms, "mp", scatter_dimension=1, tiled=True)
-    layer = (layer + hidden.reshape(tokens, width_local).astype(jnp.float32)).astype(jnp.bfloat16)
-    verified = route(layer.reshape(count, drafts, width_local), permutation, count, peers)
+    verified = output_branch(
+        gated.reshape(tokens, inner_local), out_proj, flat_hidden, permutation, count, n_mp, n_dp
+    )
     return (verified, new_state_pool, new_conv_pool)
 
 

time: 325 us -> 213 us (0.66); the launches traced: 320 us -> 212 us
  waiting for transfers between devices: 203 us -> 0.68 us
  Pallas kernels: 27.9 us -> 172 us
  blocking collectives: 32.2 us -> 0 us
  matrix products: 18.2 us -> 10.5 us
  other arithmetic: 9.33 us -> 4.17 us
  starting transfers between devices: 4.52 us -> 0.04 us
    pallas_call x0 -> x3, Pallas kernels: none -> 144 us  [the longest x1 67.1 us: gather(): pl.pallas_call(functools.partial(gather_kernel, n_mp, n_dp), out_shape=tu...]
    reduce_scatter x1 -> x0, waiting for transfers between devices: 75.2 us -> none  [on_device(): layer = lax.psum_scatter(terms, 'mp', scatter_dimension=1, tiled=True)]
    all_gather x3 -> x0, waiting for transfers between devices: 73 us -> none  [the longest x1 34.1 us: on_device(): x_weight = lax.all_gather(in_x, 'dp', axis=0, tiled=True)]
    psum x1 -> x0, waiting for transfers between devices: 33.2 us -> none  [on_device(): summed = lax.psum(partial, 'mp')]
    all_gather x3 -> x0, blocking collectives: 32.2 us -> none  [the longest x1 12.9 us: on_device(): x_proj = lax.all_gather(x_proj, 'dp', axis=0, tiled=True)]
    all_gather x1, waiting for transfers between devices: 12.9 us -> 0.01 us  [on_device(): out_proj = lax.all_gather(out_proj, 'dp', axis=1, tiled=True)]
    dot_general x1 -> x0, matrix products: 6.82 us -> none  [on_device(): jnp.dot(gated.reshape(tokens, inner_local), out_proj, preferred_element_t...]
    all_to_all x1 -> x0, waiting for transfers between devices: 5.65 us -> none  [route(): got = lax.all_to_all(sent, 'dp', split_axis=0, concat_axis=0, tiled=True)]
  transfers between devices with their start and end apart: 7 -> 1, of which waited for: 7 -> 0; matrix products, arithmetic and copies ran while one was open for 8% -> 10% of each run, Pallas kernels for 9% -> 52%
where the time goes in v2:
time: 213 us; the launch traced here: 212 us
  Pallas kernels  172 us (81%)
  between operations  14.2 us (7%)
  local copies, waits for them, and re-layouts  11 us (5%)
  matrix products  10.5 us (5%)
  other arithmetic  4.17 us (2%)
    pallas_call x1, Pallas kernels, gather(): pl.pallas_call(functools.partial(gather_kernel, n_mp, n_dp), out_shape=tu...  67.1 us
    pallas_call x1, Pallas kernels, output_branch(): pl.pallas_call(functools.partial(output_kernel, n_mp, n_dp), out_shape=ja...  60.9 us
    pallas_call x1, Pallas kernels, scan_branch(): pl.pallas_call(scan_kernel, out_shape=(jax.ShapeDtypeStruct(inputs.shape,...  23.7 us
    pallas_call x1, Pallas kernels, sum_over_mp(): pl.pallas_call(functools.partial(sum_kernel, n_mp), out_shape=jax.ShapeDt...  16.3 us
    unnamed x30, local copies, waits for them, and re-layouts  7.78 us
    dot_general x1, matrix products, on_device(): jnp.dot(normed, x_weight, preferred_element_type=jnp.float32)  5.25 us
    dot_general x1, matrix products, on_device(): jnp.dot(normed, z_weight, preferred_element_type=jnp.float32)  5.24 us
  transfers between devices with their start and end apart: 1, of which 0 were waited for; matrix products, arithmetic and copies ran while one was open for 10% of the time, Pallas kernels for 52%

profile of v2, /device:TPU:9, one launch (start us, length us, event | category | flops | bytes accessed | tf_op | source)
XLA Modules:
  0.0 212.2 jit_solution(8192652865823153177)
XLA Ops:
  7.2 0.0 all-gather.2.cloned.1.call-start
  7.2 0.7 all-gather.2.cloned.1.call-update
  7.9 1.5 copy.27.refs_4_
  9.4 1.4 copy.28.pool_ref
  10.8 1.3 broadcast_in_dim.2.refs_1_
  12.1 67.1 %shard_map.184 = (bf16[512,2048]{1,0:T(8,128)(2,1)}, bf16[4,16,512]{2,1,0:T(8,128)(2,1)}, bf16[8,256,1024]{2,1,0:T(8,128)(2,1)}, bf16[8,256,1024]{2,1,0:T(8,128)...) custom-call(bf16[512,512]{1,0:T(8,128)(2,1)} %bitcast.19, bf16[16,512]{1,0:T(8,128)(2,1)} %broadcast_in_dim.2.refs_1_, ...), custom_call_target="tpu_custom_call" | custom-call | bytes 100000000 | tf_op jit(solution)/shard_map/pallas_call | solution.py:277
  79.2 0.7 and_select_fusion.slot_ref
  79.9 2.1 fusion
  82.0 0.8 slice_convert_fusion
  82.7 0.0 copy-start.2
  82.7 0.0 copy-start.3
  82.7 0.0 copy-start.4
  82.8 0.0 copy-start.5
  82.8 5.2 %convolution_convert_fusion.1 = bf16[512,1024]{1,0:T(8,128)(2,1)S(1)} fusion(bf16[2048,1024]{1,0:T(8,128)(2,1)} %bitcast.34, bf16[512,2048]{1,0:T(8,128)(2,1)} %get-tuple-element.16, f32[2048]{0:T(1024)S(1)} %bitcast.31, f32[512]{0:T(512)S(1)} %add_rsqrt_fusion), kind=kOutput, calls=%fused_computation.6 | convolution fusion | flops 2152202240 | bytes 7350272 | tf_op jit(solution)/shard_map/dot_general | solution.py:457
  88.0 0.0 copy-done.2
  88.0 0.0 copy-done.3
  88.0 0.0 copy-done.4
  88.0 0.0 copy-done.5
  88.1 3.6 %shard_map.185 = (bf16[32,16,1024]{2,1,0:T(8,128)(2,1)S(1)}, f32[512,160]{1,0:T(8,128)S(1)}, f32[40,3,1024]{2,1,0:T(4,128)S(1)}) custom-call(s32[32]{0:T(128)S(1)} %and_select_fusion.slot_ref, s32[32]{0:T(128)S(1)} %copy-done.5, bf16[32,16,1024]{2,1,0:T(8,128)(2,1)S(1)} %bitcast.18, f32[40,3,1024]{2,1,0:T(4,128)S(1)} %copy.28.pool_ref, ...), custom_call_target="tpu_custom_call" | custom-call | flops 200000000 | bytes 4000000 | tf_op jit(solution)/shard_map/pallas_call | solution.py:47
  91.6 0.0 copy-start.1
  91.6 0.8 copy-done.1
  92.4 16.3 %shard_map.186 = bf16[512,160]{1,0:T(8,128)(2,1)} custom-call(f32[512,160]{1,0:T(8,128)} %copy-done.1), custom_call_target="tpu_custom_call" | custom-call | bytes 20000000 | tf_op jit(solution)/shard_map/pallas_call | solution.py:330
  108.8 0.9 slice.15
  109.7 0.9 slice.14
  110.6 0.1 copy.29
  110.8 1.1 copy.30
  111.8 0.0 copy-start.6
  111.8 0.0 copy-start.7
  111.8 0.0 copy-start.8
  111.8 0.0 copy-start.9
  111.9 5.2 %convolution_convert_fusion = bf16[512,1024]{1,0:T(8,128)(2,1)S(1)} fusion(bf16[2048,1024]{1,0:T(8,128)(2,1)} %bitcast.33, bf16[512,2048]{1,0:T(8,128)(2,1)} %get-tuple-element.16, f32[2048]{0:T(1024)S(1)} %bitcast.32, f32[512]{0:T(512)S(1)} %add_rsqrt_fusion), kind=kOutput, calls=%fused_computation.5 | convolution fusion | flops 2152202240 | bytes 7350272 | tf_op jit(solution)/shard_map/dot_general | solution.py:458
  117.1 0.0 copy-done.6
  117.1 0.0 copy-done.7
  117.1 0.0 copy-done.8
  117.1 0.0 copy-done.9
  117.1 0.0 copy-start.12
  117.2 0.0 copy-start
  117.2 23.7 %shard_map.187 = (bf16[32,16,1024]{2,1,0:T(8,128)(2,1)S(1)}, f32[40,16,1024]{2,1,0:T(8,128)}) custom-call(s32[32]{0:T(128)S(1)} %and_select_fusion.slot_ref, s32[32]{0:T(128)S(1)} %copy-done.5, bf16[32,16,128]{2,1,0:T(8,128)(2,1)S(1)} %bitcast.23, bf16[128,1024]{1,0:T(8,128)(2,1)S(1)} %bitcast.25, f32[1,1024]{1,0:T(1,128)S(1)} %bitcast.26, ...), custom_call_target="tpu_custom_call" | custom-call | flops 100000000 | bytes 10000000 | tf_op jit(solution)/shard_map/pallas_call | solution.py:106
  140.8 0.0 copy-start.10
  140.8 1.0 copy-done.10
  141.8 0.0 copy-done.12
  141.8 0.6 iota_reduce_fusion
  142.4 0.0 all-gather.2.cloned.1.call-done.proj_ref
  142.5 0.0 copy-done
  142.5 0.0 copy-start.11
  142.5 1.2 copy-done.11
  143.7 60.9 %shard_map.188 = bf16[32,16,512]{2,1,0:T(8,128)(2,1)S(1)} custom-call(s32[8]{0:T(128)S(1)} %and_select_fusion.1.shift_ref, s32[8]{0:T(128)S(1)} %get-tuple-element.15.class_ref, bf16[512,1024]{1,0:T(8,128)(2,1)S(1)} %bitcast.28, bf16[1024,2048]{1,0:T(8,128)(2,1)} %all-gather.2.cloned.1.call-done.proj_ref, bf16[512,512]{1,0:T(8,128)(2,1)S(1)} %bitcast.20), custom_call_target="tpu_custom_call" | custom-call | flops 2000000000 | bytes 100000000 | tf_op jit(solution)/shard_map/pallas_call | solution.py:407
  204.6 0.8 copy.32
  (2 shorter events, 0.0 us)
Async XLA Ops:
  7.2 135.3 %all-gather.2.cloned.1.call-start = ((), (), s32[]{:S(2)}) async-start(), calls=%async_computation | async-start | bytes 4718592 | tf_op jit(solution)/shard_map/all_gather | solution.py:442
  82.7 5.3 %copy-start.2 = (bf16[8,128,160]{2,1,0:T(8,128)(2,1)S(1)}, bf16[8,128,160]{2,1,0:T(8,128)(2,1)}, u32[]{:S(2)}) copy-start(bf16[8,128,160]{2,1,0:T(8,128)(2,1)} %get-tuple-element.19) | copy-start | bytes 983044
  82.7 5.3 %copy-start.3 = (f32[4,1024]{1,0:T(4,128)S(1)}, f32[4,1024]{1,0:T(4,128)}, u32[]{:S(2)}) copy-start(f32[4,1024]{1,0:T(4,128)} %weight_ref.1) | copy-start | bytes 49156
  82.7 5.3 %copy-start.4 = (f32[1024]{0:T(1024)S(1)}, f32[1024]{0:T(1024)}, u32[]{:S(2)}) copy-start(f32[1024]{0:T(1024)} %param.22) | copy-start | bytes 12292
  82.8 5.3 %copy-start.5 = (s32[32]{0:T(128)S(1)}, s32[32]{0:T(128)}, u32[]{:S(2)}) copy-start(s32[32]{0:T(128)} %accepted_ref.3) | copy-start | bytes 388
  91.6 0.8 copy-start.1
  111.8 5.3 %copy-start.6 = (bf16[8,16,1024]{2,1,0:T(8,128)(2,1)S(1)}, bf16[8,16,1024]{2,1,0:T(8,128)(2,1)}, u32[]{:S(2)}) copy-start(bf16[8,16,1024]{2,1,0:T(8,128)(2,1)} %get-tuple-element.21) | copy-start | bytes 786436
  111.8 5.3 %copy-start.7 = (f32[16,1024]{1,0:T(8,128)S(1)}, f32[16,1024]{1,0:T(8,128)}, u32[]{:S(2)}) copy-start(f32[16,1024]{1,0:T(8,128)} %a_log_ref.1) | copy-start | bytes 196612
  111.8 5.3 %copy-start.8 = (f32[1024]{0:T(1024)S(1)}, f32[1024]{0:T(1024)}, u32[]{:S(2)}) copy-start(f32[1024]{0:T(1024)} %param.25) | copy-start | bytes 12292
  111.8 5.3 %copy-start.9 = (f32[1024]{0:T(1024)S(1)}, f32[1024]{0:T(1024)}, u32[]{:S(2)}) copy-start(f32[1024]{0:T(1024)} %param.27) | copy-start | bytes 12292
  117.1 24.7 %copy-start.12 = (s32[32]{0:T(128)S(1)}, s32[32]{0:T(128)}, u32[]{:S(2)}) copy-start(s32[32]{0:T(128)} %param.31) | copy-start | bytes 388
  117.2 25.3 %copy-start = (bf16[32,16,512]{2,1,0:T(8,128)(2,1)S(1)}, bf16[32,16,512]{2,1,0:T(8,128)(2,1)}, u32[]{:S(2)}) copy-start(bf16[32,16,512]{2,1,0:T(8,128)(2,1)} %param.17) | copy-start | bytes 1572868
  140.8 1.0 copy-start.10
  142.5 1.2 copy-start.11
Sparse Core Ops, SparseCore 0:
  9.9 60.3 all-gather.1

commit v3 on v2

--- a/solution.py
+++ b/solution.py
@@ -57,72 +57,6 @@
         compiler_params=pltpu.CompilerParams(vmem_limit_bytes=VMEM_BYTES),
         cost_estimate=pl.CostEstimate(flops=200_000_000, bytes_accessed=4_000_000, transcendentals=600_000),
     )(slot, accepted, x_part, conv_pool, conv_weight, conv_bias.reshape(1, -1), x_proj)
-
-
-def scan_kernel(
-    slot_ref, accepted_ref, low_ref, proj_ref, dt_bias_ref, a_log_ref, skip_ref,
-    inputs_ref, z_ref, both_ref, pool_ref,
-    gated_ref, new_pool_ref, decay, delta, drive, rows,
-):
-    count, drafts, inner = inputs_ref.shape
-    states = a_log_ref.shape[0]
-    blocks = inner // LANES
-    new_pool_ref[...] = pool_ref[...]
-    decay[...] = -jnp.exp(a_log_ref[...])
-
-    def one(r, _):
-        slot = slot_ref[r]
-        last = accepted_ref[r] - 1
-        raw = jnp.dot(low_ref[r], proj_ref[...], preferred_element_type=jnp.float32) + dt_bias_ref[...]
-        step = jnp.maximum(raw, 0.0) + jnp.log1p(jnp.exp(-jnp.abs(raw)))
-        delta[...] = step
-        drive[...] = step * inputs_ref[r].astype(jnp.float32)
-        both = both_ref[r]
-        state = [pool_ref[slot, :, j * LANES : (j + 1) * LANES] for j in range(blocks)]
-        kept = list(state)
-        for t in range(drafts):
-            column = jnp.broadcast_to(both[:, t : t + 1], (2 * states, LANES))
-            b_wide, c_wide = column[:states], column[states:]
-            chosen = last == t
-            for j in range(blocks):
-                lanes = slice(j * LANES, (j + 1) * LANES)
-                grown = jnp.exp(delta[t : t + 1, lanes] * decay[:, lanes]) * state[j]
-                state[j] = grown + drive[t : t + 1, lanes] * b_wide
-                rows[t : t + 1, lanes] = jnp.sum(state[j] * c_wide, axis=0, keepdims=True)
-                kept[j] = jnp.where(chosen, state[j], kept[j])
-        for j in range(blocks):
-            new_pool_ref[slot, :, j * LANES : (j + 1) * LANES] = kept[j]
-        z = z_ref[r].astype(jnp.float32)
-        mixed = rows[...] + skip_ref[...] * inputs_ref[r].astype(jnp.float32)
-        gated_ref[r] = (mixed * (z / (1.0 + jnp.exp(-z)))).astype(jnp.bfloat16)
-        return 0
-
-    lax.fori_loop(0, count, one, 0)
-
-
-def scan_branch(low, dt_proj, dt_bias, a_log, skip, inputs, z_part, both, state_pool, slot, accepted):
-    count, drafts, inner = inputs.shape
-    states = a_log.shape[0]
-    return pl.pallas_call(
-        scan_kernel,
-        out_shape=(
-            jax.ShapeDtypeStruct(inputs.shape, jnp.bfloat16),
-            jax.ShapeDtypeStruct(state_pool.shape, jnp.float32),
-        ),
-        in_specs=whole(11, smem=2),
-        out_specs=tuple(whole(2)),
-        scratch_shapes=[
-            pltpu.VMEM((states, inner), jnp.float32),
-            pltpu.VMEM((drafts, inner), jnp.float32),
-            pltpu.VMEM((drafts, inner), jnp.float32),
-            pltpu.VMEM((drafts, inner), jnp.float32),
-        ],
-        compiler_params=pltpu.CompilerParams(vmem_limit_bytes=VMEM_BYTES),
-        cost_estimate=pl.CostEstimate(flops=100_000_000, bytes_accessed=10_000_000, transcendentals=9_000_000),
-    )(
-        slot, accepted, low, dt_proj, dt_bias.reshape(1, -1), a_log, skip.reshape(1, -1),
-        inputs, z_part, both, state_pool,
-    )
 
 
 MESH = pl.DeviceIdType.MESH
@@ -289,9 +223,17 @@
     )(hidden, gain, *weights)
 
 
-def sum_kernel(n_mp, partial_ref, total_ref, sent, landed, send, recv):
+def sum_kernel(n_mp, partial_ref, normed_ref, weight_ref, total_ref, z_ref, sent, landed, send, recv):
     m = lax.axis_index("mp")
     rows = partial_ref.shape[0] // n_mp
+    blocks = 4
+    width = weight_ref.shape[1] // blocks
+
+    def gate(block):
+        columns = slice(block * width, (block + 1) * width)
+        product = jnp.dot(normed_ref[...], weight_ref[:, columns], preferred_element_type=jnp.float32)
+        z_ref[:, columns] = product.astype(jnp.bfloat16)
+
     greet(peers_on("mp", n_mp))
     copies = []
     for k in range(1, n_mp):
@@ -304,6 +246,8 @@
         )
         copy.start()
         copies.append(copy)
+    for block in range(blocks // 2):
+        gate(block)
     mine = pl.ds(pl.multiple_of(m * rows, rows), rows)
     total = partial_ref[mine, :]
     for k in range(1, n_mp):
@@ -319,111 +263,199 @@
         )
         copy.start()
         spread.append(copy)
+    for block in range(blocks // 2, blocks):
+        gate(block)
     for copy in spread:
         copy.wait_recv()
     for copy in copies + spread:
         copy.wait_send()
 
 
-def sum_over_mp(partial, n_mp):
+def sum_and_gate(partial, normed, z_weight, n_mp):
     rows, columns = partial.shape
     return pl.pallas_call(
         functools.partial(sum_kernel, n_mp),
-        out_shape=jax.ShapeDtypeStruct(partial.shape, jnp.bfloat16),
-        in_specs=whole(1),
-        out_specs=whole(1)[0],
+        out_shape=(
+            jax.ShapeDtypeStruct(partial.shape, jnp.bfloat16),
+            jax.ShapeDtypeStruct((rows, z_weight.shape[1]), jnp.bfloat16),
+        ),
+        in_specs=whole(3),
+        out_specs=tuple(whole(2)),
         scratch_shapes=[
             pltpu.VMEM((n_mp - 1, rows // n_mp, columns), jnp.bfloat16),
             pltpu.VMEM((n_mp - 1, rows // n_mp, columns), jnp.bfloat16),
             pltpu.SemaphoreType.DMA((2 * (n_mp - 1),)),
             pltpu.SemaphoreType.DMA((2 * (n_mp - 1),)),
         ],
-        compiler_params=pltpu.CompilerParams(collective_id=1, has_side_effects=True),
-        cost_estimate=pl.CostEstimate(flops=0, bytes_accessed=20_000_000, transcendentals=0),
-    )(partial)
-
-
-def output_kernel(
-    n_mp, n_dp, shift_ref, class_ref, gated_ref, proj_ref, hidden_ref, out_ref,
-    sent, landed, total, rows, outgoing, incoming, send, recv,
+        compiler_params=pltpu.CompilerParams(
+            collective_id=1, has_side_effects=True, vmem_limit_bytes=VMEM_BYTES
+        ),
+        cost_estimate=pl.CostEstimate(flops=2_000_000_000, bytes_accessed=30_000_000, transcendentals=0),
+    )(partial, normed, z_weight)
+
+
+def scan_kernel(
+    n_mp, n_dp, shift_ref, class_ref, slot_ref, accepted_ref, holder_ref,
+    low_ref, dt_proj_ref, dt_bias_ref, a_log_ref, skip_ref, inputs_ref, z_ref, pool_ref,
+    proj_ref, hidden_ref,
+    out_ref, new_pool_ref,
+    decay, delta, drive, scanned, kept_ref, gated,
+    sent, landed, total, rows, outgoing, incoming, send, recv, route_send, route_recv,
 ):
     m, d = lax.axis_index("mp"), lax.axis_index("dp")
     width = hidden_ref.shape[1]
     capacity, period, drafts, _ = rows.shape
+    states, inner = a_log_ref.shape
+    rank = dt_proj_ref.shape[0]
+    part = 512
+    chunk = period * drafts
     greet(peers_on("mp", n_mp) + peers_on("dp", n_dp))
+    decay[...] = -jnp.exp(a_log_ref[...])
+
+    def scan_one(r, where):
+        slot = slot_ref[r]
+        last = accepted_ref[r] - 1
+        packed = low_ref[r]
+        raw = jnp.dot(packed[:, :rank], dt_proj_ref[...], preferred_element_type=jnp.float32)
+        raw = raw + dt_bias_ref[...]
+        step = jnp.maximum(raw, 0.0) + jnp.log1p(jnp.exp(-jnp.abs(raw)))
+        delta[...] = step
+        drive[...] = step * inputs_ref[r].astype(jnp.float32)
+        both = packed[:, rank:].astype(jnp.float32).T
+        pieces = [slice(i, i + part) for i in range(0, inner, part)]
+        state = [pool_ref[slot, :, lanes] for lanes in pieces]
+        kept = list(state)
+        for t in range(drafts):
+            column = jnp.broadcast_to(both[:, t : t + 1], (2 * states, part))
+            b_wide, c_wide = column[:states], column[states:]
+            chosen = last == t
+            for i, lanes in enumerate(pieces):
+                grown = jnp.exp(delta[t : t + 1, lanes] * decay[:, lanes]) * state[i]
+                state[i] = grown + drive[t : t + 1, lanes] * b_wide
+                scanned[t : t + 1, lanes] = jnp.sum(state[i] * c_wide, axis=0, keepdims=True)
+                kept[i] = jnp.where(chosen, state[i], kept[i])
+        for i, lanes in enumerate(pieces):
+            kept_ref[r, :, lanes] = kept[i]
+        z = z_ref[r].astype(jnp.float32)
+        mixed = scanned[...] + skip_ref[...] * inputs_ref[r].astype(jnp.float32)
+        gated[where] = (mixed * (z / (1.0 + jnp.exp(-z)))).astype(jnp.bfloat16)
 
     def share(target):
         columns = pl.ds(pl.multiple_of(target * width, width), width)
-        return jnp.dot(gated_ref[...], proj_ref[:, columns], preferred_element_type=jnp.float32)
+        flat = gated[...].reshape(chunk, inner)
+        return jnp.dot(flat, proj_ref[:, columns], preferred_element_type=jnp.float32)
 
     copies = []
-    for k in range(1, n_mp):
-        target = lax.rem(m + k, n_mp)
-        sent[k - 1] = share(target).astype(jnp.bfloat16)
-        copy = pltpu.make_async_remote_copy(
-            src_ref=sent.at[k - 1], dst_ref=landed.at[k - 1], send_sem=send.at[k - 1],
-            recv_sem=recv.at[k - 1], device_id={"mp": target}, device_id_type=MESH,
-        )
-        copy.start()
-        copies.append(copy)
-    total[...] = share(m) + hidden_ref[...].astype(jnp.float32)
-    for copy in copies:
+    for c in range(capacity):
+
+        def one(k, carry, c=c):
+            scan_one(c * period + k, k)
+            return carry
+
+        lax.fori_loop(0, period, one, 0)
+        for k in range(1, n_mp):
+            target = lax.rem(m + k, n_mp)
+            index = c * (n_mp - 1) + k - 1
+            sent[index] = share(target).astype(jnp.bfloat16)
+            copy = pltpu.make_async_remote_copy(
+                src_ref=sent.at[index], dst_ref=landed.at[index], send_sem=send.at[index],
+                recv_sem=recv.at[index], device_id={"mp": target}, device_id_type=MESH,
+            )
+            copy.start()
+            copies.append(copy)
+        own = hidden_ref[c * chunk : (c + 1) * chunk, :].astype(jnp.float32)
+        total[c] = share(m) + own
+
+    def settle(s, carry):
+        holder = holder_ref[s]
+        kept = kept_ref[jnp.maximum(holder, 0)]
+        new_pool_ref[s] = jnp.where(holder >= 0, kept, pool_ref[s])
+        return carry
+
+    lax.fori_loop(0, new_pool_ref.shape[0], settle, 0)
+    routed = []
+    for c in range(capacity):
+        layer = total[c]
+        for k in range(n_mp - 1):
+            index = c * (n_mp - 1) + k
+            copies[index].wait_recv()
+            layer = layer + landed[index].astype(jnp.float32)
+        rows[c] = layer.astype(jnp.bfloat16).reshape(period, drafts, width)
+        for o in range(n_dp):
+            if o == 0:
+                incoming[c, 0] = rows[c, class_ref[0]]
+                continue
+            outgoing[c, o] = rows[c, class_ref[o]]
+            index = c * (n_dp - 1) + o - 1
+            copy = pltpu.make_async_remote_copy(
+                src_ref=outgoing.at[c, o], dst_ref=incoming.at[c, o], send_sem=route_send.at[index],
+                recv_sem=route_recv.at[index], device_id={"dp": lax.rem(d + o, n_dp)},
+                device_id_type=MESH,
+            )
+            copy.start()
+            routed.append(copy)
+    for copy in routed:
         copy.wait_recv()
-    layer = total[...]
-    for k in range(1, n_mp):
-        layer = layer + landed[k - 1].astype(jnp.float32)
-    rows[...] = layer.astype(jnp.bfloat16).reshape(rows.shape)
-    for o in range(n_dp):
-        for c in range(capacity):
-            outgoing[o, c] = rows[c, class_ref[o]]
-        if o == 0:
-            incoming[0] = outgoing[0]
-            continue
-        index = n_mp - 2 + o
-        copy = pltpu.make_async_remote_copy(
-            src_ref=outgoing.at[o], dst_ref=incoming.at[o], send_sem=send.at[index],
-            recv_sem=recv.at[index], device_id={"dp": lax.rem(d + o, n_dp)}, device_id_type=MESH,
-        )
-        copy.start()
-        copies.append(copy)
-    for copy in copies[n_mp - 1 :]:
-        copy.wait_recv()
-    for k in range(period):
-        for c in range(capacity):
-            out_ref[c * period + k] = incoming[shift_ref[k], c]
-    for copy in copies:
+    for c in range(capacity):
+        for k in range(period):
+            out_ref[c * period + k] = incoming[c, shift_ref[k]]
+    for copy in copies + routed:
         copy.wait_send()
 
 
-def output_branch(gated, out_proj, hidden, permutation, count, n_mp, n_dp):
+def scan_and_output(
+    low, dt_proj, dt_bias, a_log, skip, inputs, z_part, state_pool, out_proj, hidden,
+    permutation, slot, accepted, n_mp, n_dp,
+):
     tokens, width = hidden.shape
-    drafts = tokens // count
+    count, drafts, inner = inputs.shape
+    states, slots = a_log.shape[0], state_pool.shape[0]
     period = min(count, n_dp)
     capacity = count // period
     shift = (permutation[:period] // count - lax.axis_index("dp") + n_dp) % n_dp
     klass = jnp.argmax(jnp.arange(n_dp)[:, None] == shift[None, :], axis=1).astype(jnp.int32)
-    box = (n_dp, capacity, drafts, width)
-    copies = n_mp - 1 + n_dp - 1
+    held = slot[None, :] == jnp.arange(slots)[:, None]
+    holder = jnp.max(jnp.where(held, jnp.arange(count)[None, :], -1), axis=1).astype(jnp.int32)
+    box = (capacity, n_dp, drafts, width)
+    sums = (capacity * (n_mp - 1), period * drafts, width)
+    routes = capacity * (n_dp - 1)
     return pl.pallas_call(
-        functools.partial(output_kernel, n_mp, n_dp),
-        out_shape=jax.ShapeDtypeStruct((count, drafts, width), jnp.bfloat16),
-        in_specs=whole(5, smem=2),
-        out_specs=whole(1)[0],
+        functools.partial(scan_kernel, n_mp, n_dp),
+        out_shape=(
+            jax.ShapeDtypeStruct((count, drafts, width), jnp.bfloat16),
+            jax.ShapeDtypeStruct(state_pool.shape, jnp.float32),
+        ),
+        in_specs=whole(15, smem=5),
+        out_specs=tuple(whole(2)),
         scratch_shapes=[
-            pltpu.VMEM((n_mp - 1, tokens, width), jnp.bfloat16),
-            pltpu.VMEM((n_mp - 1, tokens, width), jnp.bfloat16),
-            pltpu.VMEM((tokens, width), jnp.float32),
+            pltpu.VMEM((states, inner), jnp.float32),
+            pltpu.VMEM((drafts, inner), jnp.float32),
+            pltpu.VMEM((drafts, inner), jnp.float32),
+            pltpu.VMEM((drafts, inner), jnp.float32),
+            pltpu.VMEM((count, states, inner), jnp.float32),
+            pltpu.VMEM((period, drafts, inner), jnp.bfloat16),
+            pltpu.VMEM(sums, jnp.bfloat16),
+            pltpu.VMEM(sums, jnp.bfloat16),
+            pltpu.VMEM((capacity, period * drafts, width), jnp.float32),
             pltpu.VMEM((capacity, period, drafts, width), jnp.bfloat16),
             pltpu.VMEM(box, jnp.bfloat16),
             pltpu.VMEM(box, jnp.bfloat16),
-            pltpu.SemaphoreType.DMA((copies,)),
-            pltpu.SemaphoreType.DMA((copies,)),
+            pltpu.SemaphoreType.DMA((sums[0],)),
+            pltpu.SemaphoreType.DMA((sums[0],)),
+            pltpu.SemaphoreType.DMA((routes,)),
+            pltpu.SemaphoreType.DMA((routes,)),
         ],
         compiler_params=pltpu.CompilerParams(
             collective_id=2, has_side_effects=True, vmem_limit_bytes=VMEM_BYTES
         ),
-        cost_estimate=pl.CostEstimate(flops=2_000_000_000, bytes_accessed=100_000_000, transcendentals=0),
-    )(shift.astype(jnp.int32), klass, gated, out_proj, hidden)
+        cost_estimate=pl.CostEstimate(
+            flops=3_000_000_000, bytes_accessed=150_000_000, transcendentals=9_000_000
+        ),
+    )(
+        shift.astype(jnp.int32), klass, slot, accepted, holder,
+        low, dt_proj, dt_bias.reshape(1, -1), a_log, skip.reshape(1, -1),
+        inputs, z_part, state_pool, out_proj, hidden,
+    )
 
 
 def on_device(
@@ -433,13 +465,10 @@
     count, drafts, width_local = hidden.shape
     tokens = count * drafts
     inner_local = in_x.shape[1]
-    states = a_log.shape[0]
-    rank = x_proj.shape[1] - 2 * states
     slot = page_table % state_pool.shape[0]
     n_dp, n_mp = lax.axis_size("dp"), lax.axis_size("mp")
     flat_hidden = hidden.reshape(tokens, width_local)
 
-    out_proj = lax.all_gather(out_proj, "dp", axis=1, tiled=True)
     if n_dp == 8:
         weights = (in_x, in_z, x_proj, dt_proj)
         full, gain, *weights = gather(flat_hidden, norm_gain, weights, n_mp, n_dp)
@@ -450,26 +479,23 @@
             lax.all_gather(w, "dp", axis=0, tiled=True) for w in (in_x, in_z, x_proj, dt_proj)
         ]
     gain = gain[:, 0, :].reshape(-1)
+    out_proj, full = lax.optimization_barrier((out_proj, full))
+    out_proj = lax.all_gather(out_proj, "dp", axis=1, tiled=True)
 
     rows = full.astype(jnp.float32)
     scale = lax.rsqrt(jnp.mean(rows * rows, axis=1, keepdims=True) + EPS)
     normed = (rows * scale * gain.astype(jnp.float32)).astype(jnp.bfloat16)
     x_part = jnp.dot(normed, x_weight, preferred_element_type=jnp.float32).astype(jnp.bfloat16)
-    z_part = jnp.dot(normed, z_weight, preferred_element_type=jnp.float32).astype(jnp.bfloat16)
     x_part = x_part.reshape(count, drafts, inner_local)
-    z_part = z_part.reshape(count, drafts, inner_local)
 
     inputs, partial, new_conv_pool = conv_branch(
         x_part, conv_pool, conv_weight, conv_bias, x_proj, slot, accepted
     )
-    summed = sum_over_mp(partial, n_mp)
-    low = summed[:, :rank].reshape(count, drafts, rank)
-    both = summed[:, rank:].astype(jnp.float32).reshape(count, drafts, 2 * states).transpose(0, 2, 1)
-    gated, new_state_pool = scan_branch(
-        low, dt_proj, dt_bias, a_log, skip, inputs, z_part, both, state_pool, slot, accepted
-    )
-    verified = output_branch(
-        gated.reshape(tokens, inner_local), out_proj, flat_hidden, permutation, count, n_mp, n_dp
+    summed, z_part = sum_and_gate(partial, normed, z_weight, n_mp)
+    verified, new_state_pool = scan_and_output(
+        summed.reshape(count, drafts, -1), dt_proj, dt_bias, a_log, skip, inputs,
+        z_part.reshape(count, drafts, inner_local), state_pool, out_proj, flat_hidden,
+        permutation, slot, accepted, n_mp, n_dp,
     )
     return (verified, new_state_pool, new_conv_pool)
 

time: 213 us -> 178 us (0.84)
  Pallas kernels: 172 us -> 141 us
  matrix products: 10.5 us -> 2.36 us
  waiting for transfers between devices: 0.68 us -> 5.57 us
    pallas_call x3 -> x2, Pallas kernels: 101 us -> 81.3 us  [the longest x1 63.9 us: scan_and_output(): pl.pallas_call(functools.partial(scan_kernel, n_mp, n_dp), out_shape=(jax...]
    pallas_call x1, Pallas kernels: 67.1 us -> 55.8 us  [gather(): pl.pallas_call(functools.partial(gather_kernel, n_mp, n_dp), out_shape=tu...]
    all_gather x1, waiting for transfers between devices: 0.01 us -> 5.55 us  [on_device(): out_proj = lax.all_gather(out_proj, 'dp', axis=1, tiled=True)]
    dot_general x1 -> x0, matrix products: 5.24 us -> none  [on_device(): jnp.dot(normed, z_weight, preferred_element_type=jnp.float32)]
    dot_general x1, matrix products: 5.25 us -> 2.36 us  [on_device(): jnp.dot(normed, x_weight, preferred_element_type=jnp.float32)]
    unnamed x30 -> x29, local copies, waits for them, and re-layouts: 7.78 us -> 8.52 us
  transfers between devices with their start and end apart: 1 -> 1, of which waited for: 0 -> 1; matrix products, arithmetic and copies ran while one was open for 10% -> 6% of each run, Pallas kernels for 52% -> 12%
where the time goes in v3:
time: 178 us
  Pallas kernels  141 us (79%)
  between operations  14.2 us (8%)
  local copies, waits for them, and re-layouts  9.8 us (6%)
  waiting for transfers between devices  5.57 us (3%)
  other arithmetic  5.1 us (3%)
  matrix products  2.36 us (1%)
    pallas_call x1, Pallas kernels, scan_and_output(): pl.pallas_call(functools.partial(scan_kernel, n_mp, n_dp), out_shape=(jax...  63.9 us
    pallas_call x1, Pallas kernels, gather(): pl.pallas_call(functools.partial(gather_kernel, n_mp, n_dp), out_shape=tu...  55.8 us
    pallas_call x1, Pallas kernels, sum_and_gate(): pl.pallas_call(functools.partial(sum_kernel, n_mp), out_shape=(jax.ShapeD...  17.4 us
    unnamed x29, local copies, waits for them, and re-layouts  8.52 us
    all_gather x1, waiting for transfers between devices, on_device(): out_proj = lax.all_gather(out_proj, 'dp', axis=1, tiled=True)  5.55 us
    pallas_call x1, Pallas kernels, conv_branch(): pl.pallas_call(conv_kernel, out_shape=(jax.ShapeDtypeStruct(x_part.shape,...  3.75 us
  transfers between devices with their start and end apart: 1, of which 1 were waited for; matrix products, arithmetic and copies ran while one was open for 6% of the time, Pallas kernels for 12%

profile of v3, /device:TPU:9, one launch (start us, length us, event | category | flops | bytes accessed | tf_op | source)
XLA Modules:
  0.0 177.9 jit_solution(6064449696616924968)
XLA Ops:
  7.2 0.0 all-gather.2.cloned.1.call-start
  7.2 1.5 copy.23.refs_4_
  8.7 1.3 broadcast_in_dim.12.refs_1_
  10.0 55.8 %shard_map.184 = (bf16[512,2048]{1,0:T(8,128)(2,1)}, bf16[4,16,512]{2,1,0:T(8,128)(2,1)}, bf16[8,256,1024]{2,1,0:T(8,128)(2,1)}, bf16[8,256,1024]{2,1,0:T(8,128)...) custom-call(bf16[512,512]{1,0:T(8,128)(2,1)} %bitcast.15, bf16[16,512]{1,0:T(8,128)(2,1)} %broadcast_in_dim.12.refs_1_, ...), custom_call_target="tpu_custom_call" | custom-call | bytes 100000000 | tf_op jit(solution)/shard_map/pallas_call | solution.py:211
  65.8 0.0 copy-start.9
  65.8 0.0 all-gather.2.cloned.1.call-update
  65.8 1.5 copy.24.pool_ref
  67.3 0.0 copy-start.10
  67.4 0.8 and_select_fusion.slot_ref
  68.2 2.2 %fusion = f32[512]{0:T(512)S(1)} fusion(bf16[512,2048]{1,0:T(8,128)(2,1)} %get-tuple-element.21), kind=kLoop, calls=%fused_computation.2 | loop fusion | flops 3145216 | bytes 2099200 | tf_op jit(solution)/shard_map/reduce_sum | solution.py:486
  70.4 0.8 slice_convert_fusion
  71.2 0.0 copy-done.9
  71.2 0.5 fusion.2.normed_ref
  71.7 0.0 copy-done.10
  71.7 0.0 copy-start.1
  71.7 0.0 copy-start.2
  71.8 0.0 copy-start.3
  71.8 0.0 copy-start.4
  71.8 2.4 %convolution_convert_fusion = bf16[512,1024]{1,0:T(8,128)(2,1)S(1)} fusion(bf16[512,2048]{1,0:T(8,128)(2,1)S(1)} %fusion.2.normed_ref, bf16[2048,1024]{1,0:T(8,128)(2,1)S(1)} %bitcast.26), kind=kOutput, calls=%fused_computation.5 | convolution fusion | flops 2148007936 | bytes 7340032 | tf_op jit(solution)/shard_map/dot_general | solution.py:488
  74.1 0.0 copy-done.1
  74.2 0.0 copy-done.2
  74.2 0.0 copy-done.3
  74.2 0.0 copy-done.4
  74.2 3.7 %shard_map.185 = (bf16[32,16,1024]{2,1,0:T(8,128)(2,1)S(1)}, f32[512,160]{1,0:T(8,128)S(1)}, f32[40,3,1024]{2,1,0:T(4,128)S(1)}) custom-call(s32[32]{0:T(128)S(1)} %and_select_fusion.slot_ref, s32[32]{0:T(128)S(1)} %copy-done.4, bf16[32,16,1024]{2,1,0:T(8,128)(2,1)S(1)} %bitcast.14, f32[40,3,1024]{2,1,0:T(4,128)S(1)} %copy.24.pool_ref, ...), custom_call_target="tpu_custom_call" | custom-call | flops 200000000 | bytes 4000000 | tf_op jit(solution)/shard_map/pallas_call | solution.py:47
  77.9 0.0 copy-start.11
  77.9 0.0 copy-start
  78.0 0.0 copy-start.5
  78.0 0.0 copy-start.6
  78.0 0.0 copy-start.7
  78.0 0.0 copy-start.8
  78.0 1.1 copy.25
  79.1 0.1 select_reduce_fusion.holder_ref
  79.2 17.4 %shard_map.186 = (bf16[512,160]{1,0:T(8,128)(2,1)S(1)}, bf16[512,1024]{1,0:T(8,128)(2,1)S(1)}) custom-call(f32[512,160]{1,0:T(8,128)S(1)} %get-tuple-element.25.partial_ref, bf16[512,2048]{1,0:T(8,128)(2,1)S(1)} %fusion.2.normed_ref, bf16[2048,1024]{1,0:T(8,128)(2,1)} %bitcast.25), custom_call_target="tpu_custom_call" | custom-call | flops 2000000000 | bytes 30000000 | tf_op jit(solution)/shard_map/pallas_call | solution.py:276
  96.6 0.0 copy-done.11
  96.6 0.6 iota_reduce_fusion
  97.3 5.6 %all-gather.2.cloned.1.call-done.proj_ref = bf16[1024,2048]{1,0:T(8,128)(2,1)} async-done(((bf16[1024,256]{1,0:T(8,128)(2,1)}), bf16[1024,2048]{1,0:T(8,128)(2,1)}) %all-gather.2.cloned.1.call-update) | async-done | bytes 4194320 | tf_op jit(solution)/shard_map/all_gather | solution.py:483
  102.8 0.0 copy-done
  102.8 0.0 copy-done.5
  102.8 0.0 copy-done.6
  102.8 0.0 copy-done.7
  102.8 0.0 copy-done.8
  102.8 63.9 %shard_map.187 = (bf16[32,16,512]{2,1,0:T(8,128)(2,1)S(1)}, f32[40,16,1024]{2,1,0:T(8,128)}) custom-call(s32[8]{0:T(128)S(1)} %and_select_fusion.1.shift_ref, s32[8]{0:T(128)S(1)} %get-tuple-element.19.class_ref, s32[32]{0:T(128)S(1)} %and_select_fusion.slot_ref, s32[32]{0:T(128)S(1)} %copy-done.4, s32[40]{0:T(128)S(1)} %select_reduce_fusion.holder_ref, ...), custom_call_target="tpu_custom_call" | custom-call | flops 3000000000 | bytes 150000000 | tf_op jit(solution)/shard_map/pallas_call | solution.py:422
  166.7 0.8 copy.28
  167.5 3.6 %copy.29 = f32[40,16,1024]{2,1,0:T(8,128)} copy(f32[40,16,1024]{2,1,0:T(8,128)} %get-tuple-element.45) | data formatting | bytes 5242880
  (2 shorter events, 0.0 us)
Async XLA Ops:
  7.2 95.6 %all-gather.2.cloned.1.call-start = ((), (), s32[]{:S(2)}) async-start(), calls=%async_computation | async-start | bytes 4718592 | tf_op jit(solution)/shard_map/all_gather | solution.py:483
  65.8 5.4 %copy-start.9 = (bf16[512,2048]{1,0:T(8,128)(2,1)S(1)}, bf16[512,2048]{1,0:T(8,128)(2,1)}, u32[]{:S(2)}) copy-start(bf16[512,2048]{1,0:T(8,128)(2,1)} %get-tuple-element.21) | copy-start | bytes 6291460
  67.3 4.4 %copy-start.10 = (bf16[8,256,1024]{2,1,0:T(8,128)(2,1)S(1)}, bf16[8,256,1024]{2,1,0:T(8,128)(2,1)}, u32[]{:S(2)}) copy-start(bf16[8,256,1024]{2,1,0:T(8,128)(2,1)} %get-tuple-element.23) | copy-start | bytes 12582916
  71.7 2.4 %copy-start.1 = (bf16[8,128,160]{2,1,0:T(8,128)(2,1)S(1)}, bf16[8,128,160]{2,1,0:T(8,128)(2,1)}, u32[]{:S(2)}) copy-start(bf16[8,128,160]{2,1,0:T(8,128)(2,1)} %get-tuple-element.24) | copy-start | bytes 983044
  71.7 2.4 %copy-start.2 = (f32[4,1024]{1,0:T(4,128)S(1)}, f32[4,1024]{1,0:T(4,128)}, u32[]{:S(2)}) copy-start(f32[4,1024]{1,0:T(4,128)} %weight_ref.1) | copy-start | bytes 49156
  71.8 2.4 %copy-start.3 = (f32[1024]{0:T(1024)S(1)}, f32[1024]{0:T(1024)}, u32[]{:S(2)}) copy-start(f32[1024]{0:T(1024)} %param.22) | copy-start | bytes 12292
  71.8 2.4 %copy-start.4 = (s32[32]{0:T(128)S(1)}, s32[32]{0:T(128)}, u32[]{:S(2)}) copy-start(s32[32]{0:T(128)} %accepted_ref.3) | copy-start | bytes 388
  77.9 18.7 %copy-start.11 = (s32[32]{0:T(128)S(1)}, s32[32]{0:T(128)}, u32[]{:S(2)}) copy-start(s32[32]{0:T(128)} %param.31) | copy-start | bytes 388
  77.9 24.9 %copy-start = (bf16[32,16,512]{2,1,0:T(8,128)(2,1)S(1)}, bf16[32,16,512]{2,1,0:T(8,128)(2,1)}, u32[]{:S(2)}) copy-start(bf16[32,16,512]{2,1,0:T(8,128)(2,1)} %param.17) | copy-start | bytes 1572868
  78.0 24.9 %copy-start.5 = (bf16[8,16,1024]{2,1,0:T(8,128)(2,1)S(1)}, bf16[8,16,1024]{2,1,0:T(8,128)(2,1)}, u32[]{:S(2)}) copy-start(bf16[8,16,1024]{2,1,0:T(8,128)(2,1)} %get-tuple-element.28) | copy-start | bytes 786436
  78.0 24.8 %copy-start.6 = (f32[16,1024]{1,0:T(8,128)S(1)}, f32[16,1024]{1,0:T(8,128)}, u32[]{:S(2)}) copy-start(f32[16,1024]{1,0:T(8,128)} %a_log_ref.1) | copy-start | bytes 196612
  78.0 24.8 %copy-start.7 = (f32[1024]{0:T(1024)S(1)}, f32[1024]{0:T(1024)}, u32[]{:S(2)}) copy-start(f32[1024]{0:T(1024)} %param.25) | copy-start | bytes 12292
  78.0 24.8 %copy-start.8 = (f32[1024]{0:T(1024)S(1)}, f32[1024]{0:T(1024)}, u32[]{:S(2)}) copy-start(f32[1024]{0:T(1024)} %param.27) | copy-start | bytes 12292
Sparse Core Ops, SparseCore 0:
  65.9 36.8 all-gather.1

commit v4 on v3

--- a/solution.py
+++ b/solution.py
@@ -38,8 +38,16 @@
         return 0
 
     lax.fori_loop(0, count, one, 0)
-    inputs = inputs_ref[...].reshape(count * drafts, -1)
-    partial_ref[...] = jnp.dot(inputs, proj_ref[...], preferred_element_type=jnp.float32)
+    pieces, columns, depth = proj_ref.shape
+    partial_ref[...] = jnp.zeros_like(partial_ref)
+    total = None
+    for i in range(pieces):
+        part = inputs_ref[:, :, i * depth : (i + 1) * depth].reshape(count * drafts, depth)
+        term = lax.dot_general(
+            part, proj_ref[i], (((1,), (1,)), ((), ())), preferred_element_type=jnp.float32
+        )
+        total = term if total is None else total + term
+    partial_ref[:, :columns] = total
 
 
 def conv_branch(x_part, conv_pool, conv_weight, conv_bias, x_proj, slot, accepted):
@@ -48,7 +56,7 @@
         conv_kernel,
         out_shape=(
             jax.ShapeDtypeStruct(x_part.shape, jnp.bfloat16),
-            jax.ShapeDtypeStruct((count * drafts, x_proj.shape[1]), jnp.float32),
+            jax.ShapeDtypeStruct((count * drafts, 2 * LANES), jnp.float32),
             jax.ShapeDtypeStruct(conv_pool.shape, jnp.float32),
         ),
         in_specs=whole(7, smem=2),
@@ -300,7 +308,8 @@
     proj_ref, hidden_ref,
     out_ref, new_pool_ref,
     decay, delta, drive, scanned, kept_ref, gated,
-    sent, landed, total, rows, outgoing, incoming, send, recv, route_send, route_recv,
+    sent, landed, relay_out, relay_in, far_own, far_sent, far_landed, total, rows, outgoing, incoming,
+    send, recv, relay_send, relay_recv, far_send, far_recv, route_send, route_recv,
 ):
     m, d = lax.axis_index("mp"), lax.axis_index("dp")
     width = hidden_ref.shape[1]
@@ -321,7 +330,7 @@
         step = jnp.maximum(raw, 0.0) + jnp.log1p(jnp.exp(-jnp.abs(raw)))
         delta[...] = step
         drive[...] = step * inputs_ref[r].astype(jnp.float32)
-        both = packed[:, rank:].astype(jnp.float32).T
+        both = packed[:, rank : rank + 2 * states].astype(jnp.float32).T
         pieces = [slice(i, i + part) for i in range(0, inner, part)]
         state = [pool_ref[slot, :, lanes] for lanes in pieces]
         kept = list(state)
@@ -345,7 +354,27 @@
         flat = gated[...].reshape(chunk, inner)
         return jnp.dot(flat, proj_ref[:, columns], preferred_element_type=jnp.float32)
 
-    copies = []
+    partner = m + 1 - 2 * lax.rem(m, 2)
+    far = 2 - 2 * (m // 2)
+    is_end = (m == 0) | (m == n_mp - 1)
+    is_inner = (m > 0) & (m < n_mp - 1)
+    copies, relays, fars = [], [], []
+
+    def remote(src, dst, send_sem, recv_sem, target):
+        return pltpu.make_async_remote_copy(
+            src_ref=src, dst_ref=dst, send_sem=send_sem, recv_sem=recv_sem,
+            device_id={"mp": target}, device_id_type=MESH,
+        )
+
+    def pass_on(c):
+        @pl.when(is_inner)
+        def _():
+            for j in range(2):
+                relays[c][j].wait_recv()
+                mixed = far_own[c % 2, j] + relay_in[c, j].astype(jnp.float32)
+                far_sent[c, j] = mixed.astype(jnp.bfloat16)
+                fars[c][j].start()
+
     for c in range(capacity):
 
         def one(k, carry, c=c):
@@ -353,18 +382,30 @@
             return carry
 
         lax.fori_loop(0, period, one, 0)
-        for k in range(1, n_mp):
-            target = lax.rem(m + k, n_mp)
-            index = c * (n_mp - 1) + k - 1
-            sent[index] = share(target).astype(jnp.bfloat16)
-            copy = pltpu.make_async_remote_copy(
-                src_ref=sent.at[index], dst_ref=landed.at[index], send_sem=send.at[index],
-                recv_sem=recv.at[index], device_id={"mp": target}, device_id_type=MESH,
-            )
-            copy.start()
-            copies.append(copy)
+        relays.append([
+            remote(relay_out.at[c, j], relay_in.at[c, j], relay_send.at[c, j], relay_recv.at[c, j], partner)
+            for j in range(2)
+        ])
+        fars.append([
+            remote(far_sent.at[c, j], far_landed.at[c], far_send.at[c, j], far_recv.at[c], far + j)
+            for j in range(2)
+        ])
+        for j in range(2):
+            far_own[c % 2, j] = share(far + j)
+
+            @pl.when(is_end)
+            def _():
+                relay_out[c, j] = far_own[c % 2, j].astype(jnp.bfloat16)
+                relays[c][j].start()
+
+        sent[c] = share(partner).astype(jnp.bfloat16)
+        copies.append(remote(sent.at[c], landed.at[c], send.at[c], recv.at[c], partner))
+        copies[c].start()
         own = hidden_ref[c * chunk : (c + 1) * chunk, :].astype(jnp.float32)
         total[c] = share(m) + own
+        if c > 0:
+            pass_on(c - 1)
+    pass_on(capacity - 1)
 
     def settle(s, carry):
         holder = holder_ref[s]
@@ -375,11 +416,9 @@
     lax.fori_loop(0, new_pool_ref.shape[0], settle, 0)
     routed = []
     for c in range(capacity):
-        layer = total[c]
-        for k in range(n_mp - 1):
-            index = c * (n_mp - 1) + k
-            copies[index].wait_recv()
-            layer = layer + landed[index].astype(jnp.float32)
+        copies[c].wait_recv()
+        fars[c][0].wait_recv()
+        layer = total[c] + landed[c].astype(jnp.float32) + far_landed[c].astype(jnp.float32)
         rows[c] = layer.astype(jnp.bfloat16).reshape(period, drafts, width)
         for o in range(n_dp):
             if o == 0:
@@ -401,6 +440,10 @@
             out_ref[c * period + k] = incoming[c, shift_ref[k]]
     for copy in copies + routed:
         copy.wait_send()
+    for c in range(capacity):
+        for j in range(2):
+            pl.when(is_end)(relays[c][j].wait_send)
+            pl.when(is_inner)(fars[c][j].wait_send)
 
 
 def scan_and_output(
@@ -417,7 +460,7 @@
     held = slot[None, :] == jnp.arange(slots)[:, None]
     holder = jnp.max(jnp.where(held, jnp.arange(count)[None, :], -1), axis=1).astype(jnp.int32)
     box = (capacity, n_dp, drafts, width)
-    sums = (capacity * (n_mp - 1), period * drafts, width)
+    piece = (period * drafts, width)
     routes = capacity * (n_dp - 1)
     return pl.pallas_call(
         functools.partial(scan_kernel, n_mp, n_dp),
@@ -434,14 +477,23 @@
             pltpu.VMEM((drafts, inner), jnp.float32),
             pltpu.VMEM((count, states, inner), jnp.float32),
             pltpu.VMEM((period, drafts, inner), jnp.bfloat16),
-            pltpu.VMEM(sums, jnp.bfloat16),
-            pltpu.VMEM(sums, jnp.bfloat16),
+            pltpu.VMEM((capacity,) + piece, jnp.bfloat16),
+            pltpu.VMEM((capacity,) + piece, jnp.bfloat16),
+            pltpu.VMEM((capacity, 2) + piece, jnp.bfloat16),
+            pltpu.VMEM((capacity, 2) + piece, jnp.bfloat16),
+            pltpu.VMEM((2, 2) + piece, jnp.float32),
+            pltpu.VMEM((capacity, 2) + piece, jnp.bfloat16),
+            pltpu.VMEM((capacity,) + piece, jnp.bfloat16),
             pltpu.VMEM((capacity, period * drafts, width), jnp.float32),
             pltpu.VMEM((capacity, period, drafts, width), jnp.bfloat16),
             pltpu.VMEM(box, jnp.bfloat16),
             pltpu.VMEM(box, jnp.bfloat16),
-            pltpu.SemaphoreType.DMA((sums[0],)),
-            pltpu.SemaphoreType.DMA((sums[0],)),
+            pltpu.SemaphoreType.DMA((capacity,)),
+            pltpu.SemaphoreType.DMA((capacity,)),
+            pltpu.SemaphoreType.DMA((capacity, 2)),
+            pltpu.SemaphoreType.DMA((capacity, 2)),
+            pltpu.SemaphoreType.DMA((capacity, 2)),
+            pltpu.SemaphoreType.DMA((capacity,)),
             pltpu.SemaphoreType.DMA((routes,)),
             pltpu.SemaphoreType.DMA((routes,)),
         ],
@@ -470,14 +522,16 @@
     flat_hidden = hidden.reshape(tokens, width_local)
 
     if n_dp == 8:
-        weights = (in_x, in_z, x_proj, dt_proj)
+        weights = (in_x, in_z, x_proj.T, dt_proj)
         full, gain, *weights = gather(flat_hidden, norm_gain, weights, n_mp, n_dp)
-        x_weight, z_weight, x_proj, dt_proj = [w.reshape(-1, w.shape[2]) for w in weights]
+        x_weight, z_weight, _, dt_proj = [w.reshape(-1, w.shape[2]) for w in weights]
+        x_proj = weights[2]
     else:
         full, gain = gather(flat_hidden, norm_gain, (), n_mp, n_dp)
         x_weight, z_weight, x_proj, dt_proj = [
             lax.all_gather(w, "dp", axis=0, tiled=True) for w in (in_x, in_z, x_proj, dt_proj)
         ]
+        x_proj = x_proj.T[None]
     gain = gain[:, 0, :].reshape(-1)
     out_proj, full = lax.optimization_barrier((out_proj, full))
     out_proj = lax.all_gather(out_proj, "dp", axis=1, tiled=True)

time: 178 us -> 167 us (0.938)
  Pallas kernels: 141 us -> 131 us
    pallas_call x1, Pallas kernels: 63.9 us -> 54.5 us  [scan_and_output(): pl.pallas_call(functools.partial(scan_kernel, n_mp, n_dp), out_shape=(jax...]
    unnamed x29 -> x28, local copies, waits for them, and re-layouts: 8.52 us -> 7 us
  transfers between devices with their start and end apart: 1 -> 1, of which waited for: 1 -> 1; matrix products, arithmetic and copies ran while one was open for 6% -> 6% of each run, Pallas kernels for 12% -> 13%
where the time goes in v4:
time: 167 us; the launch traced here: 166 us
  Pallas kernels  131 us (78%)
  between operations  14.2 us (9%)
  local copies, waits for them, and re-layouts  8.29 us (5%)
  waiting for transfers between devices  5.47 us (3%)
  other arithmetic  5.1 us (3%)
  matrix products  2.36 us (1%)
    pallas_call x1, Pallas kernels, gather(): pl.pallas_call(functools.partial(gather_kernel, n_mp, n_dp), out_shape=tu...  55 us
    pallas_call x1, Pallas kernels, scan_and_output(): pl.pallas_call(functools.partial(scan_kernel, n_mp, n_dp), out_shape=(jax...  54.5 us
    pallas_call x1, Pallas kernels, sum_and_gate(): pl.pallas_call(functools.partial(sum_kernel, n_mp), out_shape=(jax.ShapeD...  17.4 us
    unnamed x28, local copies, waits for them, and re-layouts  7 us
    all_gather x1, waiting for transfers between devices, on_device(): out_proj = lax.all_gather(out_proj, 'dp', axis=1, tiled=True)  5.46 us
    pallas_call x1, Pallas kernels, conv_branch(): pl.pallas_call(conv_kernel, out_shape=(jax.ShapeDtypeStruct(x_part.shape,...  3.84 us
  transfers between devices with their start and end apart: 1, of which 1 were waited for; matrix products, arithmetic and copies ran while one was open for 6% of the time, Pallas kernels for 13%

profile of v4, /device:TPU:9, one launch (start us, length us, event | category | flops | bytes accessed | tf_op | source)
XLA Modules:
  0.0 166.3 jit_solution(16612721123542000127)
XLA Ops:
  7.2 0.0 all-gather.2.cloned.1.call-start
  7.2 1.3 broadcast_in_dim.12.refs_1_
  8.5 55.0 %shard_map.184 = (bf16[512,2048]{1,0:T(8,128)(2,1)}, bf16[4,16,512]{2,1,0:T(8,128)(2,1)}, bf16[8,256,1024]{2,1,0:T(8,128)(2,1)}, bf16[8,256,1024]{2,1,0:T(8,128)...) custom-call(bf16[512,512]{1,0:T(8,128)(2,1)} %bitcast.15, bf16[16,512]{1,0:T(8,128)(2,1)} %broadcast_in_dim.12.refs_1_, ...), custom_call_target="tpu_custom_call" | custom-call | bytes 100000000 | tf_op jit(solution)/shard_map/pallas_call | solution.py:219
  63.5 0.0 copy-start.9
  63.5 0.0 all-gather.2.cloned.1.call-update
  63.6 1.5 copy.22.pool_ref
  65.1 0.0 copy-start.10
  65.1 0.8 and_select_fusion.slot_ref
  65.9 2.2 %fusion = f32[512]{0:T(512)S(1)} fusion(bf16[512,2048]{1,0:T(8,128)(2,1)} %get-tuple-element.21), kind=kLoop, calls=%fused_computation.2 | loop fusion | flops 3145216 | bytes 2099200 | tf_op jit(solution)/shard_map/reduce_sum | solution.py:540
  68.1 0.8 slice_convert_fusion
  68.9 0.0 copy-done.9
  68.9 0.5 fusion.2.normed_ref
  69.5 0.0 copy-done.10
  69.5 0.0 copy-start.1
  69.5 0.0 copy-start.2
  69.5 0.0 copy-start.3
  69.5 0.0 copy-start.4
  69.5 2.4 %convolution_convert_fusion = bf16[512,1024]{1,0:T(8,128)(2,1)S(1)} fusion(bf16[512,2048]{1,0:T(8,128)(2,1)S(1)} %fusion.2.normed_ref, bf16[2048,1024]{1,0:T(8,128)(2,1)S(1)} %bitcast.26), kind=kOutput, calls=%fused_computation.5 | convolution fusion | flops 2148007936 | bytes 7340032 | tf_op jit(solution)/shard_map/dot_general | solution.py:542
  71.9 0.0 copy-done.1
  71.9 0.0 copy-done.2
  71.9 0.0 copy-done.3
  71.9 0.0 copy-done.4
  71.9 3.8 %shard_map.185 = (bf16[32,16,1024]{2,1,0:T(8,128)(2,1)S(1)}, f32[512,256]{1,0:T(8,128)S(1)}, f32[40,3,1024]{2,1,0:T(4,128)S(1)}) custom-call(s32[32]{0:T(128)S(1)} %and_select_fusion.slot_ref, s32[32]{0:T(128)S(1)} %copy-done.4, bf16[32,16,1024]{2,1,0:T(8,128)(2,1)S(1)} %bitcast.14, f32[40,3,1024]{2,1,0:T(4,128)S(1)} %copy.22.pool_ref, ...), custom_call_target="tpu_custom_call" | custom-call | flops 200000000 | bytes 4000000 | tf_op jit(solution)/shard_map/pallas_call | solution.py:55
  75.8 0.0 copy-start.11
  75.8 0.0 copy-start
  75.8 0.0 copy-start.5
  75.8 0.0 copy-start.6
  75.8 0.0 copy-start.7
  75.8 0.0 copy-start.8
  75.8 1.1 copy.23
  76.9 0.1 select_reduce_fusion.holder_ref
  77.0 17.4 %shard_map.186 = (bf16[512,256]{1,0:T(8,128)(2,1)S(1)}, bf16[512,1024]{1,0:T(8,128)(2,1)S(1)}) custom-call(f32[512,256]{1,0:T(8,128)S(1)} %get-tuple-element.25.partial_ref, bf16[512,2048]{1,0:T(8,128)(2,1)S(1)} %fusion.2.normed_ref, bf16[2048,1024]{1,0:T(8,128)(2,1)} %bitcast.25), custom_call_target="tpu_custom_call" | custom-call | flops 2000000000 | bytes 30000000 | tf_op jit(solution)/shard_map/pallas_call | solution.py:284
  94.4 0.0 copy-done.11
  94.5 0.6 iota_reduce_fusion
  95.1 5.5 %all-gather.2.cloned.1.call-done.proj_ref = bf16[1024,2048]{1,0:T(8,128)(2,1)} async-done(((bf16[1024,256]{1,0:T(8,128)(2,1)}), bf16[1024,2048]{1,0:T(8,128)(2,1)}) %all-gather.2.cloned.1.call-update) | async-done | bytes 4194320 | tf_op jit(solution)/shard_map/all_gather | solution.py:537
  100.5 0.0 copy-done
  100.6 0.0 copy-done.5
  100.6 0.0 copy-done.6
  100.6 0.0 copy-done.7
  100.6 0.0 copy-done.8
  100.6 54.5 %shard_map.187 = (bf16[32,16,512]{2,1,0:T(8,128)(2,1)S(1)}, f32[40,16,1024]{2,1,0:T(8,128)}) custom-call(s32[8]{0:T(128)S(1)} %and_select_fusion.1.shift_ref, s32[8]{0:T(128)S(1)} %get-tuple-element.19.class_ref, s32[32]{0:T(128)S(1)} %and_select_fusion.slot_ref, s32[32]{0:T(128)S(1)} %copy-done.4, s32[40]{0:T(128)S(1)} %select_reduce_fusion.holder_ref, ...), custom_call_target="tpu_custom_call" | custom-call | flops 3000000000 | bytes 150000000 | tf_op jit(solution)/shard_map/pallas_call | solution.py:465
  155.1 0.8 copy.26
  155.9 3.6 %copy.27 = f32[40,16,1024]{2,1,0:T(8,128)} copy(f32[40,16,1024]{2,1,0:T(8,128)} %get-tuple-element.45) | data formatting | bytes 5242880
  (2 shorter events, 0.0 us)
Async XLA Ops:
  7.2 93.4 %all-gather.2.cloned.1.call-start = ((), (), s32[]{:S(2)}) async-start(), calls=%async_computation | async-start | bytes 4718592 | tf_op jit(solution)/shard_map/all_gather | solution.py:537
  63.5 5.4 %copy-start.9 = (bf16[512,2048]{1,0:T(8,128)(2,1)S(1)}, bf16[512,2048]{1,0:T(8,128)(2,1)}, u32[]{:S(2)}) copy-start(bf16[512,2048]{1,0:T(8,128)(2,1)} %get-tuple-element.21) | copy-start | bytes 6291460
  65.1 4.4 %copy-start.10 = (bf16[8,256,1024]{2,1,0:T(8,128)(2,1)S(1)}, bf16[8,256,1024]{2,1,0:T(8,128)(2,1)}, u32[]{:S(2)}) copy-start(bf16[8,256,1024]{2,1,0:T(8,128)(2,1)} %get-tuple-element.23) | copy-start | bytes 12582916
  69.5 2.4 %copy-start.1 = (bf16[8,160,128]{2,1,0:T(8,128)(2,1)S(1)}, bf16[8,160,128]{2,1,0:T(8,128)(2,1)}, u32[]{:S(2)}) copy-start(bf16[8,160,128]{2,1,0:T(8,128)(2,1)} %get-tuple-element.24.proj_ref) | copy-start | bytes 983044
  69.5 2.4 %copy-start.2 = (f32[4,1024]{1,0:T(4,128)S(1)}, f32[4,1024]{1,0:T(4,128)}, u32[]{:S(2)}) copy-start(f32[4,1024]{1,0:T(4,128)} %weight_ref.1) | copy-start | bytes 49156
  69.5 2.4 %copy-start.3 = (f32[1024]{0:T(1024)S(1)}, f32[1024]{0:T(1024)}, u32[]{:S(2)}) copy-start(f32[1024]{0:T(1024)} %param.22) | copy-start | bytes 12292
  69.5 2.4 %copy-start.4 = (s32[32]{0:T(128)S(1)}, s32[32]{0:T(128)}, u32[]{:S(2)}) copy-start(s32[32]{0:T(128)} %accepted_ref.3) | copy-start | bytes 388
  75.8 18.7 %copy-start.11 = (s32[32]{0:T(128)S(1)}, s32[32]{0:T(128)}, u32[]{:S(2)}) copy-start(s32[32]{0:T(128)} %param.31) | copy-start | bytes 388
  75.8 24.8 %copy-start = (bf16[32,16,512]{2,1,0:T(8,128)(2,1)S(1)}, bf16[32,16,512]{2,1,0:T(8,128)(2,1)}, u32[]{:S(2)}) copy-start(bf16[32,16,512]{2,1,0:T(8,128)(2,1)} %param.17) | copy-start | bytes 1572868
  75.8 24.8 %copy-start.5 = (bf16[8,16,1024]{2,1,0:T(8,128)(2,1)S(1)}, bf16[8,16,1024]{2,1,0:T(8,128)(2,1)}, u32[]{:S(2)}) copy-start(bf16[8,16,1024]{2,1,0:T(8,128)(2,1)} %get-tuple-element.28) | copy-start | bytes 786436
  75.8 24.8 %copy-start.6 = (f32[16,1024]{1,0:T(8,128)S(1)}, f32[16,1024]{1,0:T(8,128)}, u32[]{:S(2)}) copy-start(f32[16,1024]{1,0:T(8,128)} %a_log_ref.1) | copy-start | bytes 196612
  75.8 24.7 %copy-start.7 = (f32[1024]{0:T(1024)S(1)}, f32[1024]{0:T(1024)}, u32[]{:S(2)}) copy-start(f32[1024]{0:T(1024)} %param.25) | copy-start | bytes 12292
  75.8 24.7 %copy-start.8 = (f32[1024]{0:T(1024)S(1)}, f32[1024]{0:T(1024)}, u32[]{:S(2)}) copy-start(f32[1024]{0:T(1024)} %param.27) | copy-start | bytes 12292
Sparse Core Ops, SparseCore 0:
  63.7 36.8 all-gather.1

commit v5 on v4

--- a/solution.py
+++ b/solution.py
@@ -38,16 +38,15 @@
         return 0
 
     lax.fori_loop(0, count, one, 0)
-    pieces, columns, depth = proj_ref.shape
-    partial_ref[...] = jnp.zeros_like(partial_ref)
+    pieces, _, depth = proj_ref.shape
     total = None
     for i in range(pieces):
         part = inputs_ref[:, :, i * depth : (i + 1) * depth].reshape(count * drafts, depth)
         term = lax.dot_general(
-            part, proj_ref[i], (((1,), (1,)), ((), ())), preferred_element_type=jnp.float32
+            proj_ref[i], part, (((1,), (1,)), ((), ())), preferred_element_type=jnp.float32
         )
         total = term if total is None else total + term
-    partial_ref[:, :columns] = total
+    partial_ref[...] = total
 
 
 def conv_branch(x_part, conv_pool, conv_weight, conv_bias, x_proj, slot, accepted):
@@ -56,7 +55,7 @@
         conv_kernel,
         out_shape=(
             jax.ShapeDtypeStruct(x_part.shape, jnp.bfloat16),
-            jax.ShapeDtypeStruct((count * drafts, 2 * LANES), jnp.float32),
+            jax.ShapeDtypeStruct((x_proj.shape[1], count * drafts), jnp.float32),
             jax.ShapeDtypeStruct(conv_pool.shape, jnp.float32),
         ),
         in_specs=whole(7, smem=2),
@@ -84,13 +83,14 @@
 
 def gather_kernel(n_mp, n_dp, *refs):
     weights = 4 if n_dp == 8 else 0
-    hidden, gain = refs[0], refs[1]
+    hidden, gain_row = refs[0], refs[1]
     shards = refs[2 : 2 + weights]
-    full, gains = refs[2 + weights], refs[3 + weights]
-    wholes = refs[4 + weights : 4 + 2 * weights]
-    send, recv, local = refs[4 + 2 * weights :]
+    normed = refs[2 + weights]
+    wholes = refs[3 + weights : 3 + 2 * weights]
+    full, gain, gains, send, recv, local = refs[3 + 2 * weights :]
     m = lax.axis_index("mp")
     width = hidden.shape[1]
+    gain[...] = jnp.broadcast_to(gain_row[...].astype(jnp.float32), gain.shape)
     greet(peers_on("mp", n_mp) + (peers_on("dp", n_dp) if weights else []))
     made = []
 
@@ -153,17 +153,18 @@
         core, by_x, by_y = other(1), other(2), other(4)
         diagonal = by_x + 4 - 8 * lax.rem(d // 4, 2)
         own = []
-        for w in range(2):
+        relayed_weights = (0, 2, 1)
+        for w in relayed_weights:
             shard, whole_w = shards[w], wholes[w]
             own.append([started(shard, whole_w.at[d], {"dp": t}) for t in (by_x, by_y, core)])
             keep(shard, whole_w.at[d])
-    for k in range(1, n_mp):
-        started(gain, gains.at[m], {"mp": lax.rem(m + k, n_mp)})
+    gain_copies = {
+        id(started(gain, gains.at[m], {"mp": lax.rem(m + k, n_mp)})) for k in range(1, n_mp)
+    }
     if weights:
-        for w in range(2, 4):
-            keep(shards[w], wholes[w].at[d])
-            for k in range(1, n_dp):
-                started(shards[w], wholes[w].at[d], {"dp": lax.rem(d + k, n_dp)})
+        keep(shards[3], wholes[3].at[d])
+        for k in range(1, n_dp):
+            started(shards[3], wholes[3].at[d], {"dp": lax.rem(d + k, n_dp)})
     relay_arrive(0)
     relay_start(1)
     done = {id(copy) for pair in relay for copy in pair}
@@ -174,31 +175,53 @@
 
     if weights:
         halves = []
-        for w in range(2):
+        for i, w in enumerate(relayed_weights):
             whole_w = wholes[w]
             half = whole_w.shape[1] // 2
             low, high = pl.ds(0, half), pl.ds(half, half)
-            arrive(own[w][0])
+            arrive(own[i][0])
             first = started(whole_w.at[by_x, low], whole_w.at[by_x, low], {"dp": by_y})
             started(whole_w.at[by_x], whole_w.at[by_x], {"dp": core})
-            arrive(own[w][1])
+            arrive(own[i][1])
             second = started(whole_w.at[by_y, high], whole_w.at[by_y, high], {"dp": by_x})
             started(whole_w.at[by_y], whole_w.at[by_y], {"dp": core})
             halves.append((first, second))
-            if w == 0:
+            if i == 0:
                 relay_arrive(1)
                 relay_start(2)
-        for w in range(2):
+        for i, w in enumerate(relayed_weights):
             whole_w = wholes[w]
             half = whole_w.shape[1] // 2
-            for copy, part in zip(halves[w], (pl.ds(0, half), pl.ds(half, half))):
+            for copy, part in zip(halves[i], (pl.ds(0, half), pl.ds(half, half))):
                 arrive(copy)
                 started(whole_w.at[diagonal, part], whole_w.at[diagonal, part], {"dp": core})
     else:
         relay_arrive(1)
         relay_start(2)
     relay_arrive(2)
-    for copy in made:
+    kept[0].wait()
+    kept[1].wait()
+    for copy in made[relayed:]:
+        if id(copy) in gain_copies:
+            arrive(copy)
+    block = 64
+
+    def norm(i, carry):
+        rows = pl.ds(pl.multiple_of(i * block, block), block)
+        parts = [slice(p * width, (p + 1) * width) for p in range(n_mp)]
+        squares = None
+        for part in parts:
+            values = full[rows, part].astype(jnp.float32)
+            term = jnp.sum(values * values, axis=1, keepdims=True)
+            squares = term if squares is None else squares + term
+        scale = lax.rsqrt(squares / (n_mp * width) + EPS)
+        for p, part in enumerate(parts):
+            values = full[rows, part].astype(jnp.float32) * scale * gains[p, 0:1, :]
+            normed[rows, part] = values.astype(jnp.bfloat16)
+        return carry
+
+    lax.fori_loop(0, full.shape[0] // block, norm, 0)
+    for copy in made[relayed:]:
         if id(copy) not in done:
             copy.wait_recv()
     for s in range(steps):
@@ -206,34 +229,41 @@
             pl.when(go)(copy.wait_send)
     for copy in made[relayed:]:
         copy.wait_send()
-    for copy in kept:
+    for copy in kept[2:]:
         copy.wait()
 
 
 def gather(hidden, gain, weights, n_mp, n_dp):
     tokens, width = hidden.shape
-    gain = jnp.broadcast_to(gain[None, :], (16, width))
-    shapes = [(tokens, n_mp * width), (n_mp, 16, width)] + [(n_dp,) + w.shape for w in weights]
+    shapes = [(tokens, n_mp * width)] + [(n_dp,) + w.shape for w in weights]
     anywhere = pl.BlockSpec(memory_space=pl.ANY)
-    copies = 2 * (n_mp - 1) + n_mp - 1 + (2 * (3 + 4 + 2) + 2 * (n_dp - 1) if weights else 0)
+    copies = 2 * (n_mp - 1) + n_mp - 1 + (3 * (3 + 4 + 2) + n_dp - 1 if weights else 0)
     return pl.pallas_call(
         functools.partial(gather_kernel, n_mp, n_dp),
         out_shape=tuple(jax.ShapeDtypeStruct(s, jnp.bfloat16) for s in shapes),
-        in_specs=[anywhere] * (2 + len(weights)),
-        out_specs=tuple([anywhere] * len(shapes)),
+        in_specs=whole(2) + [anywhere] * len(weights),
+        out_specs=tuple(whole(1) + [anywhere] * len(weights)),
         scratch_shapes=[
+            pltpu.VMEM((tokens, n_mp * width), jnp.bfloat16),
+            pltpu.VMEM((8, width), jnp.float32),
+            pltpu.VMEM((n_mp, 8, width), jnp.float32),
             pltpu.SemaphoreType.DMA((copies,)),
             pltpu.SemaphoreType.DMA((copies,)),
             pltpu.SemaphoreType.DMA((2 + len(weights),)),
         ],
-        compiler_params=pltpu.CompilerParams(collective_id=0, has_side_effects=True),
+        compiler_params=pltpu.CompilerParams(
+            collective_id=0, has_side_effects=True, vmem_limit_bytes=16 * 1024 * 1024
+        ),
         cost_estimate=pl.CostEstimate(flops=0, bytes_accessed=100_000_000, transcendentals=0),
-    )(hidden, gain, *weights)
-
-
-def sum_kernel(n_mp, partial_ref, normed_ref, weight_ref, total_ref, z_ref, sent, landed, send, recv):
+    )(hidden, gain.reshape(1, -1), *weights)
+
+
+def sum_kernel(
+    n_mp, partial_ref, normed_ref, weight_ref, packed_ref, z_ref, sent, landed, total_ref, send, recv
+):
     m = lax.axis_index("mp")
-    rows = partial_ref.shape[0] // n_mp
+    columns_all, tokens = partial_ref.shape
+    rows = tokens // n_mp
     blocks = 4
     width = weight_ref.shape[1] // blocks
 
@@ -246,7 +276,7 @@
     copies = []
     for k in range(1, n_mp):
         target = lax.rem(m + k, n_mp)
-        piece = partial_ref[pl.ds(pl.multiple_of(target * rows, rows), rows), :]
+        piece = partial_ref[:, pl.ds(pl.multiple_of(target * rows, rows), rows)]
         sent[k - 1] = piece.astype(jnp.bfloat16)
         copy = pltpu.make_async_remote_copy(
             src_ref=sent.at[k - 1], dst_ref=landed.at[k - 1], send_sem=send.at[k - 1],
@@ -257,15 +287,15 @@
     for block in range(blocks // 2):
         gate(block)
     mine = pl.ds(pl.multiple_of(m * rows, rows), rows)
-    total = partial_ref[mine, :]
+    total = partial_ref[:, mine]
     for k in range(1, n_mp):
         copies[k - 1].wait_recv()
         total = total + landed[k - 1].astype(jnp.float32)
-    total_ref[mine, :] = total.astype(jnp.bfloat16)
+    total_ref[:, mine] = total.astype(jnp.bfloat16)
     spread = []
     for k in range(1, n_mp):
         copy = pltpu.make_async_remote_copy(
-            src_ref=total_ref.at[mine], dst_ref=total_ref.at[mine],
+            src_ref=total_ref.at[:, mine], dst_ref=total_ref.at[:, mine],
             send_sem=send.at[n_mp - 2 + k], recv_sem=recv.at[n_mp - 2 + k],
             device_id={"mp": lax.rem(m + k, n_mp)}, device_id_type=MESH,
         )
@@ -275,23 +305,25 @@
         gate(block)
     for copy in spread:
         copy.wait_recv()
+    packed_ref[:, :columns_all] = total_ref[...].astype(jnp.float32).T.astype(jnp.bfloat16)
     for copy in copies + spread:
         copy.wait_send()
 
 
 def sum_and_gate(partial, normed, z_weight, n_mp):
-    rows, columns = partial.shape
+    columns, rows = partial.shape
     return pl.pallas_call(
         functools.partial(sum_kernel, n_mp),
         out_shape=(
-            jax.ShapeDtypeStruct(partial.shape, jnp.bfloat16),
+            jax.ShapeDtypeStruct((rows, columns), jnp.bfloat16),
             jax.ShapeDtypeStruct((rows, z_weight.shape[1]), jnp.bfloat16),
         ),
         in_specs=whole(3),
         out_specs=tuple(whole(2)),
         scratch_shapes=[
-            pltpu.VMEM((n_mp - 1, rows // n_mp, columns), jnp.bfloat16),
-            pltpu.VMEM((n_mp - 1, rows // n_mp, columns), jnp.bfloat16),
+            pltpu.VMEM((n_mp - 1, columns, rows // n_mp), jnp.bfloat16),
+            pltpu.VMEM((n_mp - 1, columns, rows // n_mp), jnp.bfloat16),
+            pltpu.VMEM((columns, rows), jnp.bfloat16),
             pltpu.SemaphoreType.DMA((2 * (n_mp - 1),)),
             pltpu.SemaphoreType.DMA((2 * (n_mp - 1),)),
         ],
@@ -523,22 +555,18 @@
 
     if n_dp == 8:
         weights = (in_x, in_z, x_proj.T, dt_proj)
-        full, gain, *weights = gather(flat_hidden, norm_gain, weights, n_mp, n_dp)
+        normed, *weights = gather(flat_hidden, norm_gain, weights, n_mp, n_dp)
         x_weight, z_weight, _, dt_proj = [w.reshape(-1, w.shape[2]) for w in weights]
         x_proj = weights[2]
     else:
-        full, gain = gather(flat_hidden, norm_gain, (), n_mp, n_dp)
+        normed, = gather(flat_hidden, norm_gain, (), n_mp, n_dp)
         x_weight, z_weight, x_proj, dt_proj = [
             lax.all_gather(w, "dp", axis=0, tiled=True) for w in (in_x, in_z, x_proj, dt_proj)
         ]
         x_proj = x_proj.T[None]
-    gain = gain[:, 0, :].reshape(-1)
-    out_proj, full = lax.optimization_barrier((out_proj, full))
+    out_proj, normed = lax.optimization_barrier((out_proj, normed))
     out_proj = lax.all_gather(out_proj, "dp", axis=1, tiled=True)
 
-    rows = full.astype(jnp.float32)
-    scale = lax.rsqrt(jnp.mean(rows * rows, axis=1, keepdims=True) + EPS)
-    normed = (rows * scale * gain.astype(jnp.float32)).astype(jnp.bfloat16)
     x_part = jnp.dot(normed, x_weight, preferred_element_type=jnp.float32).astype(jnp.bfloat16)
     x_part = x_part.reshape(count, drafts, inner_local)
 

time: 167 us -> 168 us (level)
  Pallas kernels: 131 us -> 116 us
  local copies, waits for them, and re-layouts: 8.29 us -> 19.6 us
  waiting for transfers between devices: 5.47 us -> 12 us
  other arithmetic: 5.1 us -> 0.75 us
  matrix products: 2.36 us -> 4.53 us
    unnamed x28 -> x44, local copies, waits for them, and re-layouts: 7 us -> 18.9 us
    pallas_call x1, Pallas kernels: 55 us -> 45.4 us  [gather(): pl.pallas_call(functools.partial(gather_kernel, n_mp, n_dp), out_shape=tu...]
    all_gather x1, waiting for transfers between devices: 5.46 us -> 12 us  [on_device(): out_proj = lax.all_gather(out_proj, 'dp', axis=1, tiled=True)]
    pallas_call x1, Pallas kernels: 17.4 us -> 12.6 us  [sum_and_gate(): pl.pallas_call(functools.partial(sum_kernel, n_mp), out_shape=(jax.ShapeD...]
    reduce_sum x1 -> x0, other arithmetic: 2.21 us -> none  [on_device(): scale = lax.rsqrt(jnp.mean(rows * rows, axis=1, keepdims=True) + EPS)]
    dot_general x1, matrix products: 2.36 us -> 4.53 us  [on_device(): jnp.dot(normed, x_weight, preferred_element_type=jnp.float32)]
  transfers between devices with their start and end apart: 1 -> 1, of which waited for: 1 -> 1; matrix products, arithmetic and copies ran while one was open for 6% -> 5% of each run, Pallas kernels for 13% -> 10%
where the time goes in v5:
time: 168 us; the launch traced here: 167 us
  Pallas kernels  116 us (69%)
  local copies, waits for them, and re-layouts  19.6 us (12%)
  between operations  14.2 us (8%)
  waiting for transfers between devices  12 us (7%)
  matrix products  4.53 us (3%)
    pallas_call x1, Pallas kernels, scan_and_output(): pl.pallas_call(functools.partial(scan_kernel, n_mp, n_dp), out_shape=(jax...  54.5 us
    pallas_call x1, Pallas kernels, gather(): pl.pallas_call(functools.partial(gather_kernel, n_mp, n_dp), out_shape=tu...  45.4 us
    unnamed x44, local copies, waits for them, and re-layouts  18.9 us
    pallas_call x1, Pallas kernels, sum_and_gate(): pl.pallas_call(functools.partial(sum_kernel, n_mp), out_shape=(jax.ShapeD...  12.6 us
    all_gather x1, waiting for transfers between devices, on_device(): out_proj = lax.all_gather(out_proj, 'dp', axis=1, tiled=True)  12 us
    dot_general x1, matrix products, on_device(): jnp.dot(normed, x_weight, preferred_element_type=jnp.float32)  4.53 us
    pallas_call x1, Pallas kernels, conv_branch(): pl.pallas_call(conv_kernel, out_shape=(jax.ShapeDtypeStruct(x_part.shape,...  3.59 us
  transfers between devices with their start and end apart: 1, of which 1 were waited for; matrix products, arithmetic and copies ran while one was open for 5% of the time, Pallas kernels for 10%

profile of v5, /device:TPU:9, one launch (start us, length us, event | category | flops | bytes accessed | tf_op | source)
XLA Modules:
  0.0 167.3 jit_solution(13529439974738783651)
XLA Ops:
  7.2 0.0 copy-start.18
  7.2 0.0 all-gather.2.cloned.1.call-start
  7.2 0.7 reshape.42.refs_1_
  7.9 1.0 copy-done
  8.9 1.0 copy-done.1
  10.0 1.0 copy-done.2
  11.0 0.8 copy-done.4
  11.8 0.8 copy-done.5
  12.6 45.4 %shard_map.184 = (bf16[512,2048]{1,0:T(8,128)(2,1)S(1)}, bf16[8,256,1024]{2,1,0:T(8,128)(2,1)S(1)}, bf16[8,256,1024]{2,1,0:T(8,128)(2,1)S(1)}, bf16[8,160,128]{2,1,0:T(8,128)(2,1)S(1)}, bf16[8,16,1024]{2,1,0:T(8,128)(2,1)S(1)}) custom-call(bf16[512,512]{1,0:T(8,128)(2,1)S(1)} %bitcast.14, bf16[1,512]{1,0:T(2,128)(2,1)S(1)} %reshape.42.refs_1_, ...), custom_call_target="tpu_custom_call" | custom-call | bytes 100000000 | tf_op jit(solution)/shard_map/pallas_call | solution.py:241
  58.0 0.0 copy-start.9
  58.0 2.0 %copy-done.9 = bf16[8,256,1024]{2,1,0:T(8,128)(2,1)} copy-done((bf16[8,256,1024]{2,1,0:T(8,128)(2,1)}, bf16[8,256,1024]{2,1,0:T(8,128)(2,1)S(1)}, u32[]{:S(2)}) %copy-start.9) | copy-done | bytes 4194328
  60.0 2.0 %copy-done.10 = bf16[8,256,1024]{2,1,0:T(8,128)(2,1)} copy-done((bf16[8,256,1024]{2,1,0:T(8,128)(2,1)}, bf16[8,256,1024]{2,1,0:T(8,128)(2,1)S(1)}, u32[]{:S(2)}) %copy-start.10) | copy-done | bytes 4194328
  62.0 0.0 all-gather.2.cloned.1.call-update
  62.0 1.4 copy.22.pool_ref
  63.4 0.0 copy-done.18
  63.4 0.0 copy-start.6
  63.4 0.0 copy-start.7
  63.4 0.0 copy-start.8
  63.4 4.5 %convolution_convert_fusion = bf16[512,1024]{1,0:T(8,128)(2,1)S(1)} fusion(bf16[512,2048]{1,0:T(8,128)(2,1)S(1)} %get-tuple-element.20.normed_ref, bf16[2048,1024]{1,0:T(8,128)(2,1)} %bitcast.19), kind=kOutput, calls=%fused_computation | convolution fusion | flops 2148007936 | bytes 7340032 | tf_op jit(solution)/shard_map/dot_general | solution.py:570
  68.0 0.0 copy-done.6
  68.0 0.0 copy-done.7
  68.0 0.0 copy-done.8
  68.0 3.6 %shard_map.185 = (bf16[32,16,1024]{2,1,0:T(8,128)(2,1)S(1)}, f32[160,512]{1,0:T(8,128)S(1)}, f32[40,3,1024]{2,1,0:T(4,128)S(1)}) custom-call(s32[32]{0:T(128)S(1)} %and_select_fusion.slot_ref, s32[32]{0:T(128)S(1)} %copy-done.8, bf16[32,16,1024]{2,1,0:T(8,128)(2,1)S(1)} %bitcast.13, f32[40,3,1024]{2,1,0:T(4,128)S(1)} %copy.22.pool_ref, ...), custom_call_target="tpu_custom_call" | custom-call | flops 200000000 | bytes 4000000 | tf_op jit(solution)/shard_map/pallas_call | solution.py:54
  71.6 0.0 copy-start.11
  71.6 1.1 copy.23
  72.7 0.1 select_reduce_fusion.holder_ref
  72.8 0.0 copy-done.11
  72.8 0.0 copy-start.19
  72.8 0.0 copy-start.3
  72.8 0.0 copy-start.13
  72.8 0.0 copy-start.14
  72.9 0.0 copy-start.15
  72.9 12.6 %shard_map.186 = (bf16[512,160]{1,0:T(8,128)(2,1)S(1)}, bf16[512,1024]{1,0:T(8,128)(2,1)S(1)}) custom-call(f32[160,512]{1,0:T(8,128)S(1)} %get-tuple-element.23.partial_ref, bf16[512,2048]{1,0:T(8,128)(2,1)S(1)} %get-tuple-element.20.normed_ref, bf16[2048,1024]{1,0:T(8,128)(2,1)} %bitcast.18), custom_call_target="tpu_custom_call" | custom-call | flops 2000000000 | bytes 30000000 | tf_op jit(solution)/shard_map/pallas_call | solution.py:315
  85.5 0.0 copy-start.16
  85.5 1.0 copy-done.16
  86.5 0.0 copy-done.19
  86.5 0.6 iota_reduce_fusion
  87.1 12.0 %all-gather.2.cloned.1.call-done.proj_ref = bf16[1024,2048]{1,0:T(8,128)(2,1)} async-done(((bf16[1024,256]{1,0:T(8,128)(2,1)}), bf16[1024,2048]{1,0:T(8,128)(2,1)}) %all-gather.2.cloned.1.call-update) | async-done | bytes 4194320 | tf_op jit(solution)/shard_map/all_gather | solution.py:568
  99.1 0.0 copy-done.3
  99.1 0.0 copy-done.13
  99.1 0.0 copy-done.14
  99.2 0.0 copy-done.15
  99.2 0.0 copy-start.12
  99.2 1.2 copy-done.12
  100.4 1.2 copy-done.17
  101.6 54.5 %shard_map.187 = (bf16[32,16,512]{2,1,0:T(8,128)(2,1)S(1)}, f32[40,16,1024]{2,1,0:T(8,128)}) custom-call(s32[8]{0:T(128)S(1)} %and_select_fusion.1.shift_ref, s32[8]{0:T(128)S(1)} %get-tuple-element.18.class_ref, s32[32]{0:T(128)S(1)} %and_select_fusion.slot_ref, s32[32]{0:T(128)S(1)} %copy-done.8, s32[40]{0:T(128)S(1)} %select_reduce_fusion.holder_ref, ...), custom_call_target="tpu_custom_call" | custom-call | flops 3000000000 | bytes 150000000 | tf_op jit(solution)/shard_map/pallas_call | solution.py:497
  156.1 0.8 copy.26
  156.9 3.6 %copy.27 = f32[40,16,1024]{2,1,0:T(8,128)} copy(f32[40,16,1024]{2,1,0:T(8,128)} %get-tuple-element.43) | data formatting | bytes 5242880
  (9 shorter events, 0.0 us)
Async XLA Ops:
  7.2 56.2 %copy-start.18 = (s32[32]{0:T(128)S(1)}, s32[32]{0:T(128)}, u32[]{:S(2)}) copy-start(s32[32]{0:T(128)} %param.32) | copy-start | bytes 388
  7.2 92.0 %all-gather.2.cloned.1.call-start = ((), (), s32[]{:S(2)}) async-start(), calls=%async_computation | async-start | bytes 4718592 | tf_op jit(solution)/shard_map/all_gather | solution.py:568
  7.9 1.0 copy-start
  8.9 1.0 copy-start.1
  10.0 1.0 copy-start.2
  11.0 0.8 copy-start.4
  11.8 0.8 copy-start.5
  58.0 2.0 %copy-start.9 = (bf16[8,256,1024]{2,1,0:T(8,128)(2,1)}, bf16[8,256,1024]{2,1,0:T(8,128)(2,1)S(1)}, u32[]{:S(2)}) copy-start(bf16[8,256,1024]{2,1,0:T(8,128)(2,1)S(1)} %get-tuple-element.24) | copy-start | bytes 12582916
  60.0 2.0 %copy-start.10 = (bf16[8,256,1024]{2,1,0:T(8,128)(2,1)}, bf16[8,256,1024]{2,1,0:T(8,128)(2,1)S(1)}, u32[]{:S(2)}) copy-start(bf16[8,256,1024]{2,1,0:T(8,128)(2,1)S(1)} %get-tuple-element.21) | copy-start | bytes 12582916
  63.4 4.6 %copy-start.6 = (f32[4,1024]{1,0:T(4,128)S(1)}, f32[4,1024]{1,0:T(4,128)}, u32[]{:S(2)}) copy-start(f32[4,1024]{1,0:T(4,128)} %weight_ref.1) | copy-start | bytes 49156
  63.4 4.6 %copy-start.7 = (f32[1024]{0:T(1024)S(1)}, f32[1024]{0:T(1024)}, u32[]{:S(2)}) copy-start(f32[1024]{0:T(1024)} %param.22) | copy-start | bytes 12292
  63.4 4.6 %copy-start.8 = (s32[32]{0:T(128)S(1)}, s32[32]{0:T(128)}, u32[]{:S(2)}) copy-start(s32[32]{0:T(128)} %accepted_ref.3) | copy-start | bytes 388
  71.6 1.2 copy-start.11
  72.8 13.7 %copy-start.19 = (s32[32]{0:T(128)S(1)}, s32[32]{0:T(128)}, u32[]{:S(2)}) copy-start(s32[32]{0:T(128)} %param.31) | copy-start | bytes 388
  72.8 26.3 %copy-start.3 = (bf16[32,16,512]{2,1,0:T(8,128)(2,1)S(1)}, bf16[32,16,512]{2,1,0:T(8,128)(2,1)}, u32[]{:S(2)}) copy-start(bf16[32,16,512]{2,1,0:T(8,128)(2,1)} %param.17) | copy-start | bytes 1572868
  72.8 26.3 %copy-start.13 = (f32[16,1024]{1,0:T(8,128)S(1)}, f32[16,1024]{1,0:T(8,128)}, u32[]{:S(2)}) copy-start(f32[16,1024]{1,0:T(8,128)} %a_log_ref.1) | copy-start | bytes 196612
  72.8 26.3 %copy-start.14 = (f32[1024]{0:T(1024)S(1)}, f32[1024]{0:T(1024)}, u32[]{:S(2)}) copy-start(f32[1024]{0:T(1024)} %param.25) | copy-start | bytes 12292
  72.9 26.3 %copy-start.15 = (f32[1024]{0:T(1024)S(1)}, f32[1024]{0:T(1024)}, u32[]{:S(2)}) copy-start(f32[1024]{0:T(1024)} %param.27) | copy-start | bytes 12292
  85.5 1.0 copy-start.16
  99.2 1.2 copy-start.12
  100.4 1.2 copy-start.17
Sparse Core Ops, SparseCore 0:
  62.1 37.0 all-gather.1
